TPU v7x, 256 devices: a whole 4x4x8 slice. The times are simulated.
256 devices in a mesh: blk: 64 (over z, y, core), vec: 4 (over x).
Axes of the slice: x: 4, y: 4, z: 8, core: 2. Of those that a mesh axis runs over, the one named last changes fastest.
Arguments:
- vectors: float32 [8, 128, 5, 2, 64, 128], P('vec', 'blk'), may hold values from -15 to 15
- metric: float32 [128, 2, 64, 128], P('blk'), may hold values from 0.5 to 2
- jacobians: float32 [3, 5, 5], replicated, may hold values from -2 to 2
- block_rows: int32 [128], P('blk'), may hold values from 32 to 64, as said below
- neighbours: int32 [128, 2], P('blk'), may hold values from 0 to 127, as said below
- flipped: int32 [128, 2], P('blk'), may hold values from 0 to 1, as said below
Outputs:
- basis: float32 [8, 128, 5, 2, 64, 128], P('vec', 'blk')
- factor: float32 [8, 8], replicated
Inputs may be any that keep to these rules, and one draw needn't show every extreme that they name: Rows from block_rows[b] on are padding; some block has 64 live rows and some 64 // 2. neighbours[b, 1] is the block whose first row faces the last live row of b, and neighbours[neighbours[b, 1], 0] = b; following neighbours[., 1] from any block visits all 128 blocks in one cycle. flipped[b, 1] = flipped[neighbours[b, 1], 0].
All inputs are finite; a program needn't handle non-finite values.
Results may differ from a plain program's by a relative error of at most 0.0003.
Values sent between devices are 32-bit elements; how exact they have to be, the bound alone decides.
A program may use at most 192 MiB of HBM per device.

v0:
```python
import jax
import jax.numpy as jnp
from jax import lax
from jax.sharding import PartitionSpec as P

viscous = 0.1
epsilon = 1e-06
hardest = lax.Precision.HIGHEST


def turn_sign():
    return jnp.array([1.0, -1.0, 1.0, 1.0, 1.0], jnp.float32)


def block_faces(field_state, row_counts):
    low_face = field_state[:, :, :, :, 0, :]
    last_index = (row_counts - 1)[None, :, None, None, None, None]
    full_shape = field_state.shape[:4] + (1,) + field_state.shape[5:]
    high_face = jnp.take_along_axis(field_state, jnp.broadcast_to(last_index, full_shape), axis=4)[
        :, :, :, :, 0, :
    ]
    return jnp.stack([low_face, high_face], axis=2)


def orient(face_cells, face_flags):
    turned = jnp.flip(face_cells, -1) * turn_sign()[None, None, :, None, None]
    return jnp.where(face_flags[None, :, None, None, None] > 0, turned, face_cells)


def ghosts_from(everyone, neighbours, flipped):
    ghost_low = orient(jnp.take(everyone, neighbours[:, 0], axis=1)[:, :, 1], flipped[:, 0])
    ghost_high = orient(jnp.take(everyone, neighbours[:, 1], axis=1)[:, :, 0], flipped[:, 1])
    return (ghost_low, ghost_high)


def local_update(field_state, ghost_low, ghost_high, row_counts, jacobians, metric):
    height = field_state.shape[4]
    row_index = jnp.arange(height, dtype=jnp.int32)
    alive_mask = (row_index[None, :] < row_counts[:, None]).astype(jnp.float32)[
        None, :, None, None, :, None
    ]
    top_row = (row_index[None, :] == row_counts[:, None] - 1).astype(jnp.float32)[
        None, :, None, None, :, None
    ]
    first_row = (row_index == 0).astype(jnp.float32)[None, None, None, None, :, None]
    zero_row = jnp.zeros_like(field_state[:, :, :, :, :1, :])
    above_cells = (
        jnp.concatenate([field_state[:, :, :, :, 1:, :], zero_row], axis=4)
        + top_row * ghost_high[:, :, :, :, None, :]
    )
    below_cells = (
        jnp.concatenate([zero_row, field_state[:, :, :, :, :-1, :]], axis=4)
        + first_row * ghost_low[:, :, :, :, None, :]
    )
    zero_layer = jnp.zeros_like(field_state[:, :, :, :1])
    deeper = jnp.concatenate([field_state[:, :, :, 1:], zero_layer], axis=3)
    shallower = jnp.concatenate([zero_layer, field_state[:, :, :, :-1]], axis=3)
    right_cells = jnp.roll(field_state, -1, axis=5)
    left_cells = jnp.roll(field_state, 1, axis=5)
    flux_sum = jnp.einsum(
        "fg,vbgkji->vbfkji", jacobians[0], right_cells - left_cells, precision=hardest
    )
    flux_sum = flux_sum + jnp.einsum(
        "fg,vbgkji->vbfkji", jacobians[1], above_cells - below_cells, precision=hardest
    )
    flux_sum = flux_sum + jnp.einsum(
        "fg,vbgkji->vbfkji", jacobians[2], deeper - shallower, precision=hardest
    )
    spread = (
        right_cells
        + left_cells
        + above_cells
        + below_cells
        + deeper
        + shallower
        - 6.0 * field_state
    )
    return alive_mask * (field_state - metric[None, :, None] * flux_sum + viscous * spread)


def advance(field_state, row_counts, neighbours, flipped, jacobians, metric):
    faces = block_faces(field_state, row_counts)
    everyone = lax.all_gather(faces, "blk", axis=1, tiled=True)
    ghost_low, ghost_high = ghosts_from(everyone, neighbours, flipped)
    return local_update(field_state, ghost_low, ghost_high, row_counts, jacobians, metric)


def gram_terms(field_state, all_count, offset):
    everyone = lax.all_gather(field_state, "vec", axis=0, tiled=True)
    flat_all = everyone.reshape(all_count, -1)
    own_rows = field_state.reshape(field_state.shape[0], -1)
    partial_rows = jnp.dot(own_rows, flat_all.T, precision=hardest)
    gram_part = lax.dynamic_update_slice(
        jnp.zeros((all_count, all_count), jnp.float32), partial_rows, (offset, 0)
    )
    return (gram_part, flat_all)


def finish(mixer, kept_data, full_shape, offset):
    own_count = full_shape[0]
    own_mixer = lax.dynamic_slice_in_dim(mixer, offset, own_count, 0)
    return jnp.dot(own_mixer, kept_data, precision=hardest).reshape(full_shape)


def per_device(vectors, metric, jacobians, block_rows, neighbours, flipped):
    row_index = jnp.arange(vectors.shape[4], dtype=jnp.int32)
    alive_mask = (row_index[None, :] < block_rows[:, None]).astype(jnp.float32)[
        None, :, None, None, :, None
    ]
    start = vectors * alive_mask
    first = advance(start, block_rows, neighbours, flipped, jacobians, metric)
    own_squares = jnp.sum(first * first, axis=(1, 2, 3, 4, 5))
    own_count = first.shape[0]
    all_count = own_count * lax.axis_size("vec")
    offset = lax.axis_index("vec") * own_count
    vector_norms = jnp.sqrt(lax.psum(own_squares, "blk") + epsilon)
    scaled = first / vector_norms[:, None, None, None, None, None]
    second = advance(scaled, block_rows, neighbours, flipped, jacobians, metric)
    gram_part, kept_data = gram_terms(second, all_count, offset)
    gram_matrix = lax.psum(gram_part, ("blk", "vec"))
    column_scale = jnp.ones((all_count,), jnp.float32)
    lower_factor = jnp.linalg.cholesky(gram_matrix)
    inverse = jax.scipy.linalg.solve_triangular(
        lower_factor, jnp.eye(all_count, dtype=jnp.float32), lower=True
    )
    basis = finish(inverse * column_scale[None, :], kept_data, second.shape, offset)
    return (basis, lower_factor.T)


def solution(mesh):
    in_specs = (
        P("vec", "blk", None, None, None, None),
        P("blk", None, None, None),
        P(),
        P("blk"),
        P("blk", None),
        P("blk", None),
    )
    out_specs = (P("vec", "blk", None, None, None, None), P())
    return jax.shard_map(
        per_device, mesh=mesh, in_specs=in_specs, out_specs=out_specs, check_vma=False
    )
```

profile of v0, /device:TPU:4, one launch (start us, length us, event | category | flops | bytes accessed | tf_op | source)
XLA Modules:
  0.0 632.6 jit_solution(12793382025260153011)
XLA Ops:
  7.2 0.7 broadcast_compare_fusion
  7.9 0.7 compare_convert_fusion.2
  8.6 0.7 broadcast_add_fusion.1
  9.5 2.1 copy_multiply_fusion
  11.6 55.3 %gather_fusion = f32[5120]{0:T(1024)S(1)} fusion(f32[2,2,5,2,64,128]{5,2,4,3,1,0:T(8,128)S(1)} %copy_multiply_fusion, s32[5120]{0:T(1024)S(1)} %bitcast.106), kind=kCustom, calls=%fused_computation.clone | custom fusion | bytes 163840 | tf_op jit(solution)/shard_map/jit(take_along_axis)/gather | solution.py:19
  67.0 0.6 pad_maximum_fusion.8
  67.8 0.2 slice_reduce_fusion.1
  68.0 0.7 compare_reduce_fusion.2
  68.8 0.5 compare_and_fusion
  69.3 0.1 fusion.90
  69.5 1.0 copy-done.11
  70.4 3.2 fusion.2
  73.7 0.7 fusion.89
  74.4 0.7 fusion.88
  75.1 0.6 copy-done.4
  75.7 0.6 copy-done.6
  76.3 4.1 fusion.34
  80.4 2.3 fusion.87
  82.8 67.1 %all-gather.4.cloned.1.call-done = f32[2,128,2,5,2,128]{5,3,4,1,0,2:T(8,128)} async-done(((f32[2,2,2,5,2,128]{5,3,4,1,0,2:T(8,128)}), f32[2,128,2,5,2,128]{5,3,4,1,0,2:T(8,128)}) %all-gather.4.cloned.1.call-update) | async-done | bytes 2621456 | tf_op jit(solution)/shard_map/all_gather | solution.py:83
  149.9 5.2 copy.63
  155.1 2.3 gather_fusion.1
  157.4 0.1 fusion.52
  157.6 2.7 gather_fusion.2
  160.3 0.7 select_bitcast_fusion
  161.1 0.7 multiply_select_fusion.3
  161.8 11.2 %multiply_reduce_fusion = (f32[2]{0:T(128)S(1)}, f32[2,2,5,2,64,128]{5,2,4,3,1,0:T(8,128)}) fusion(f32[2,2,5,1,64,128]{5,2,4,3,1,0:T(8,128)} %copy-done.11, f32[2,2,5,1,64,128]{5,2,4,3,1,0:T(8,128)S(1)} %get-tuple-element.28, f32[64]{0:T(128)S(1)} %compare_convert_fusion, f32[2,2,5,2,63,128]{5,2,4,3,1,0:T(8,128)} %get-tuple-element.23, ...), kind=kOutput, calls=%fused_computation.42 | convolution fusion | flops 28835838 | bytes 11928940 | tf_op jit(solution)/shard_map/fg,vbgkji->vbfkji/dot_general | solution.py:63
  173.0 126.8 %psum.14 = f32[2]{0:T(128)S(1)} all-reduce(f32[2]{0:T(128)S(1)} %get-tuple-element.41), channel_id=1, replica_groups=mesh['blk'=64,'vec'=4] {'blk'}, use_global_device_ids=true, to_apply=%region_1.0 | all-reduce | flops 2 | bytes 16 | tf_op jit(solution)/shard_map/psum | solution.py:116
  299.8 1.8 broadcast_divide_fusion
  301.6 55.3 %gather_fusion.3 = f32[5120]{0:T(1024)S(1)} fusion(f32[2,2,5,2,64,128]{5,2,4,3,1,0:T(8,128)S(1)} %broadcast_divide_fusion, s32[5120]{0:T(1024)S(1)} %bitcast.107), kind=kCustom, calls=%fused_computation.2.clone | custom fusion | bytes 163840 | tf_op jit(solution)/shard_map/jit(take_along_axis)/gather | solution.py:19
  357.0 0.1 fusion.65
  357.1 0.6 pad_maximum_fusion.9
  357.8 0.1 fusion.86
  357.9 1.0 copy-done.10
  358.9 3.3 fusion.7
  362.2 0.7 fusion.85
  362.9 0.7 fusion.84
  363.6 0.6 copy-done
  364.2 0.6 copy-done.1
  364.8 4.1 fusion.22
  368.9 2.3 fusion.83
  371.3 62.7 %all-gather.6.cloned.1.call-done = f32[2,128,2,5,2,128]{5,3,4,1,0,2:T(8,128)} async-done(((f32[2,2,2,5,2,128]{5,3,4,1,0,2:T(8,128)}), f32[2,128,2,5,2,128]{5,3,4,1,0,2:T(8,128)}) %all-gather.6.cloned.1.call-update) | async-done | bytes 2621456 | tf_op jit(solution)/shard_map/all_gather | solution.py:83
  434.0 5.0 copy.72
  439.0 2.3 gather_fusion.5
  441.3 2.5 gather_fusion.4
  443.8 0.1 fusion.51
  444.0 0.1 rev.16
  444.1 0.1 rev.15
  444.2 0.1 multiply_select_fusion.1
  444.2 9.9 %fusion.11 = f32[2,2,5,2,64,128]{5,2,4,3,1,0:T(8,128)S(1)} fusion(f32[2,2,5,1,64,128]{5,2,4,3,1,0:T(8,128)} %copy-done.10, f32[2,2,5,1,64,128]{5,2,4,3,1,0:T(8,128)S(1)} %get-tuple-element.20, f32[2,2,5,2,64,128]{5,2,4,3,1,0:T(8,128)S(1)} %broadcast_divide_fusion, f32[2,2,2,64,128,5]{4,5,3,2,1,0:T(8,128)} %fusion.7, f32[2,2,2,64,128,5]{4,5,3,2,1,0:T(8,128)} %fusion.22, ...), kind=kOutput, calls=%fused_computation.24 | convolution fusion | flops 27852800 | bytes 11928932 | tf_op jit(solution)/shard_map/fg,vbgkji->vbfkji/dot_general | solution.py:63
  454.1 1.3 copy-done.9
  455.5 1.3 copy.78
  456.8 56.1 %all-gather.8.cloned.1.call-done = f32[8,2,5,2,64,128]{5,4,3,2,1,0:T(8,128)} async-done(((f32[2,2,5,2,64,128]{5,4,3,2,1,0:T(8,128)}), f32[8,2,5,2,64,128]{5,4,3,2,1,0:T(8,128)}) %all-gather.8.cloned.1.call-update) | async-done | bytes 5242896 | tf_op jit(solution)/shard_map/all_gather | solution.py:89
  512.9 15.3 %fusion.37 = f32[2,8]{0,1:T(8,128)S(1)} fusion(f32[8,2,5,2,64,128]{5,4,3,2,1,0:T(8,128)} %all-gather.8.cloned.1.call-done, f32[2,2,5,2,64,128]{5,2,4,3,1,0:T(8,128)} %copy-done.9), kind=kOutput, calls=%fused_computation.54 | convolution fusion | flops 31457280 | bytes 6553664 | tf_op jit(solution)/shard_map/dot_general | solution.py:92
  528.2 0.4 dynamic_update_slice.3
  528.6 75.6 %psum.15 = f32[8,8]{0,1:T(8,128)S(1)} all-reduce(f32[8,8]{0,1:T(8,128)S(1)} %dynamic_update_slice.3), channel_id=1, replica_groups=mesh['blk'=64,'vec'=4] {'blk','vec'}, use_global_device_ids=true, to_apply=%region_2.5 | all-reduce | flops 64 | bytes 512 | tf_op jit(solution)/shard_map/psum | solution.py:120
  604.2 9.4 %copy.153 = f32[1,8,1280,128]{3,1,2,0:T(8,128)} copy(f32[1,8,1280,128]{3,2,1,0:T(8,128)} %bitcast.108) | data formatting | bytes 10485760
  613.7 0.7 cholesky.16
  614.5 0.1 select_reduce_fusion
  614.6 0.6 compare_reduce_fusion
  615.3 1.2 fusion.72
  616.6 0.6 custom-call.7
  617.2 0.2 fusion.68
  617.4 7.2 %fusion.73 = f32[2,2,5,2,64,128]{5,0,4,3,2,1:T(2,128)S(1)} fusion(f32[2,5,2,64,128,8]{4,5,3,2,1,0:T(8,128)} %bitcast.109, f32[8,8]{1,0:T(8,128)S(1)} %fusion.68, s32[]{:T(128)S(6)} %select_n.40), kind=kOutput, calls=%fused_computation.139 | convolution fusion | flops 31457280 | bytes 6554628 | tf_op jit(solution)/shard_map/dot_general | solution.py:102
  624.6 1.2 copy.87
  (87 shorter events, 1.1 us)
Async XLA Ops:
  7.2 142.7 %all-gather.4.cloned.1.call-start = ((), (), s32[]{:S(2)}) async-start(), calls=%async_computation | async-start | bytes 4259840 | tf_op jit(solution)/shard_map/all_gather | solution.py:83
  7.9 59.1 %copy-start.15 = (pred[2]{0:T(512)(128)(4,1)}, pred[2]{0:T(512)(128)(4,1)S(1)}, u32[]{:S(2)}) copy-start(pred[2]{0:T(512)(128)(4,1)S(1)} %broadcast_compare_fusion) | copy-start | bytes 10
  9.3 57.7 %copy-start.19 = (s32[2]{0:T(128)}, s32[2]{0:T(128)S(1)}, u32[]{:S(2)}) copy-start(s32[2]{0:T(128)S(1)} %get-tuple-element.40) | copy-start | bytes 28
  9.3 59.5 %copy-start.17 = (s32[2]{0:T(128)}, s32[2]{0:T(128)S(1)}, u32[]{:S(2)}) copy-start(s32[2]{0:T(128)S(1)} %get-tuple-element.39) | copy-start | bytes 28
  11.6 56.2 %copy-start.26 = (s32[2,2]{1,0:T(2,128)S(1)}, s32[2,2]{1,0:T(2,128)}, u32[]{:S(2)}) copy-start(s32[2,2]{1,0:T(2,128)} %param.18) | copy-start | bytes 52
  11.6 56.4 %copy-start.27 = (s32[2,2]{1,0:T(2,128)S(1)}, s32[2,2]{1,0:T(2,128)}, u32[]{:S(2)}) copy-start(s32[2,2]{1,0:T(2,128)} %param.19) | copy-start | bytes 52
  11.6 57.7 %copy-start.14 = (f32[3,5,5]{2,0,1:T(4,128)S(1)}, f32[3,5,5]{2,0,1:T(4,128)}, u32[]{:S(2)}) copy-start(f32[3,5,5]{2,0,1:T(4,128)} %param.16) | copy-start | bytes 904
  67.7 366.2 %all-gather.6.cloned.1.call-start = ((), (), s32[]{:S(2)}) async-start(), calls=%async_computation.1 | async-start | bytes 4259840 | tf_op jit(solution)/shard_map/all_gather | solution.py:83
  68.0 87.1 %copy-start.13 = (s32[1024]{0:T(1024)}, s32[1024]{0:T(1024)S(1)}, u32[]{:S(2)}) copy-start(s32[1024]{0:T(1024)S(1)} %pad_clamp_fusion.1) | copy-start | bytes 12292
  69.3 88.1 %copy-start.24 = (pred[2]{0:T(512)(128)(4,1)}, pred[2]{0:T(512)(128)(4,1)S(1)}, u32[]{:S(2)}) copy-start(pred[2]{0:T(512)(128)(4,1)S(1)} %get-tuple-element.46) | copy-start | bytes 10
  69.5 1.0 copy-start.11
  74.3 1.4 copy-start.4
  74.4 1.9 copy-start.6
  75.1 5.3 copy-start.7
  75.1 5.3 copy-start.8
  82.8 79.1 %copy-start.12 = (f32[2,2,64,128]{3,2,1,0:T(8,128)S(1)}, f32[2,2,64,128]{3,2,1,0:T(8,128)}, u32[]{:S(2)}) copy-start(f32[2,2,64,128]{3,2,1,0:T(8,128)} %param.15) | copy-start | bytes 393220
  149.9 11.9 %copy-start.5 = (f32[2,2,5,2,64,1]{5,2,4,3,1,0:T(8,128)S(1)}, f32[2,2,5,2,64,1]{5,2,4,3,1,0:T(8,128)}, u32[]{:S(2)}) copy-start(f32[2,2,5,2,64,1]{5,2,4,3,1,0:T(8,128)} %copy-done.4) | copy-start | bytes 30724
  301.6 55.4 %copy-start.16 = (pred[2]{0:T(512)(128)(4,1)S(1)}, pred[2]{0:T(512)(128)(4,1)}, u32[]{:S(2)}) copy-start(pred[2]{0:T(512)(128)(4,1)} %copy-done.15) | copy-start | bytes 10
  301.6 55.4 %copy-start.18 = (s32[2]{0:T(128)S(1)}, s32[2]{0:T(128)}, u32[]{:S(2)}) copy-start(s32[2]{0:T(128)} %copy-done.17) | copy-start | bytes 28
  301.6 55.4 %copy-start.20 = (s32[2]{0:T(128)S(1)}, s32[2]{0:T(128)}, u32[]{:S(2)}) copy-start(s32[2]{0:T(128)} %copy-done.19) | copy-start | bytes 28
  357.7 155.2 %all-gather.8.cloned.1.call-start = ((), (), s32[]{:S(2)}) async-start(), calls=%async_computation.2 | async-start | bytes 6553600 | tf_op jit(solution)/shard_map/all_gather | solution.py:89
  357.9 1.0 copy-start.10
  362.9 1.3 copy-start
  362.9 1.9 copy-start.1
  363.6 5.3 copy-start.2
  363.6 5.3 copy-start.3
  371.3 72.6 %copy-start.25 = (pred[2]{0:T(512)(128)(4,1)S(1)}, pred[2]{0:T(512)(128)(4,1)}, u32[]{:S(2)}) copy-start(pred[2]{0:T(512)(128)(4,1)} %copy-done.24) | copy-start | bytes 10
  371.3 72.6 %copy-start.23 = (pred[2]{0:T(512)(128)(4,1)S(1)}, pred[2]{0:T(512)(128)(4,1)}, u32[]{:S(2)}) copy-start(pred[2]{0:T(512)(128)(4,1)} %get-tuple-element.45) | copy-start | bytes 10
  371.3 72.9 %copy-start.21 = (pred[2]{0:T(512)(128)(4,1)S(1)}, pred[2]{0:T(512)(128)(4,1)}, u32[]{:S(2)}) copy-start(pred[2]{0:T(512)(128)(4,1)} %get-tuple-element.10) | copy-start | bytes 10
  371.3 72.9 %copy-start.22 = (pred[2]{0:T(512)(128)(4,1)S(1)}, pred[2]{0:T(512)(128)(4,1)}, u32[]{:S(2)}) copy-start(pred[2]{0:T(512)(128)(4,1)} %get-tuple-element.11) | copy-start | bytes 10
  371.3 72.9 %copy-start.28 = (f32[5]{0:T(128)S(1)}, f32[5]{0:T(128)}, u32[]{:S(2)}) copy-start(f32[5]{0:T(128)} %constant.92.clone) | copy-start | bytes 64
  454.1 1.3 copy-start.9
Sparse Core Ops, SparseCore 0:
  67.8 81.9 all-gather.3
  357.8 76.0 all-gather.5
  456.9 55.9 all-gather.7
where the time goes:
time: 645 us; the launch traced here: 633 us
  blocking collectives  202 us (31%)
  waiting for transfers between devices  186 us (29%)
  local copies, waits for them, and re-layouts  157 us (24%)
  matrix products  58.5 us (9%)
  between operations  14.5 us (2%)
  other arithmetic  13.9 us (2%)
    all_gather x2, waiting for transfers between devices, advance(): everyone = lax.all_gather(faces, 'blk', axis=1, tiled=True)  130 us
    psum x1, blocking collectives, per_device(): vector_norms = jnp.sqrt(lax.psum(own_squares, 'blk') + epsilon)  127 us
    gather x3, local copies, waits for them, and re-layouts, block_faces(): jnp.take_along_axis(field_state, jnp.broadcast_to(last_index, full_shape)...  111 us
    psum x1, blocking collectives, per_device(): gram_matrix = lax.psum(gram_part, ('blk', 'vec'))  75.6 us
    all_gather x1, waiting for transfers between devices, gram_terms(): everyone = lax.all_gather(field_state, 'vec', axis=0, tiled=True)  56.1 us
    dot_general x2, matrix products, local_update(): jnp.einsum('fg,vbgkji->vbfkji', jacobians[1], above_cells - below_cells,...  21 us
    unnamed x65, local copies, waits for them, and re-layouts  16.4 us
    dot_general x1, matrix products, gram_terms(): partial_rows = jnp.dot(own_rows, flat_all.T, precision=hardest)  15.3 us
  transfers between devices with their start and end apart: 3, of which 3 were waited for; matrix products, arithmetic and copies ran while one was open for 4% of the time, Pallas kernels for 0%

commit v1 on v0

v1 whole, which is shorter than its diff:
```python
import jax
import jax.numpy as jnp
from jax import lax
from jax.experimental import pallas as pl
from jax.experimental.pallas import tpu as pltpu
from jax.sharding import PartitionSpec as P

MESH = pl.DeviceIdType.MESH
F32 = jnp.float32
HI = lax.Precision.HIGHEST
NF = 5
NZ, NY, NC, NX = 8, 4, 2, 4
NR = NY * NC
VISC = 0.1
EPS = 1e-06
SCALE = 1024.0


def pair(v, w):
    return v * (v + 1) // 2 + w


def kernel(vec, met, jac, rows, nbr, flip, out, fac,
           st, fi, se, gath, bas, rel1, rel2, pay, zb, rq, rqs, o2, rb, own, gst, cs, cb, gacc, ar, arx, ary, arz, spl, mix,
           loc_sem, xs, xr, fs, fr, zs, zr, qs, qr, ys, yr, cs_s, cs_r, as_s, as_r, os, orr):
    blk = lax.axis_index("blk")
    x = lax.axis_index("vec")
    z = blk // NR
    rho = lax.rem(blk, NR)
    c = lax.rem(blk, NC)
    col = lax.rem(blk, NR)

    def zdev(dz, core):
        zz = lax.rem(z + dz + NZ, NZ)
        return zz * NR + (rho - c) + core

    bar = pltpu.get_barrier_semaphore()
    n_part = 0
    for d in range(1, NX):
        pl.semaphore_signal(bar, inc=1, device_id={"blk": blk, "vec": lax.rem(x + d, NX)}, device_id_type=MESH)
        n_part += 1
    for d in range(1, NR):
        pl.semaphore_signal(bar, inc=1, device_id={"blk": z * NR + lax.rem(rho + d, NR), "vec": x}, device_id_type=MESH)
        n_part += 1
    for d in range(1, NZ):
        pl.semaphore_signal(bar, inc=1, device_id={"blk": zdev(d, c), "vec": x}, device_id_type=MESH)
        n_part += 1
    for d in (1, NZ - 1):
        pl.semaphore_signal(bar, inc=1, device_id={"blk": zdev(d, 1 - c), "vec": x}, device_id_type=MESH)
        n_part += 1

    def rcopy(src, dst, ssem, rsem, b_, x_):
        return pltpu.make_async_remote_copy(src_ref=src, dst_ref=dst, send_sem=ssem, recv_sem=rsem,
                                            device_id={"blk": b_, "vec": x_}, device_id_type=MESH)

    iota64 = lax.broadcasted_iota(jnp.int32, (64, 128), 0)
    iota8 = lax.broadcasted_iota(jnp.int32, (8, 128), 0)
    lane8 = lax.broadcasted_iota(jnp.int32, (8, 128), 1)
    zero8 = jnp.zeros((8, 128), F32)

    def fill(i, _):
        vb = i // 10
        v, b = vb // 2, lax.rem(vb, 2)
        fk = lax.rem(i, 10)
        f, k = fk // 2, lax.rem(fk, 2)
        q = vec[v, b, f, k]
        st[v, b, f, k, 8:72, :] = jnp.where(iota64 < rows[b], q, 0.0)
        st[v, b, f, k, 0:8, :] = zero8
        st[v, b, f, k, 72:80, :] = zero8
        fi[v, b, f, k, 0:8, :] = zero8
        fi[v, b, f, k, 72:80, :] = zero8
        return 0

    lax.fori_loop(0, 40, fill, 0)

    def advance_tile(src, v, b, t, scale, store):
        r0 = pl.multiple_of(t * 8, 8)
        alive = (iota8 + r0) < rows[b]
        qs_, d0, d1, base = [], [], [], []
        for k in range(2):
            qk = [src[v, b, f, k, pl.ds(r0 + 8, 8), :] for f in range(NF)]
            qs_.append(qk)
        for k in range(2):
            a0, a1, ab = [], [], []
            for f in range(NF):
                q = qs_[k][f]
                e = pltpu.roll(q, 127, 1)
                w = pltpu.roll(q, 1, 1)
                n = src[v, b, f, k, pl.ds(r0 + 9, 8), :]
                s = src[v, b, f, k, pl.ds(r0 + 7, 8), :]
                a0.append(e - w)
                a1.append(n - s)
                ab.append((scale * (1.0 - 6.0 * VISC)) * q + (scale * VISC) * ((e + w) + (n + s) + qs_[1 - k][f]))
            d0.append(a0)
            d1.append(a1)
            base.append(ab)
        mk = [met[b, k, pl.ds(r0, 8), :] * scale for k in range(2)]
        for f in range(NF):
            c0 = [jac[0, f, g] for g in range(NF)]
            c1 = [jac[1, f, g] for g in range(NF)]
            c2 = [jac[2, f, g] for g in range(NF)]
            for k in range(2):
                acc = c0[0] * d0[k][0] + c1[0] * d1[k][0]
                oth = c2[0] * qs_[1 - k][0]
                for g in range(1, NF):
                    acc = acc + c0[g] * d0[k][g] + c1[g] * d1[k][g]
                    oth = oth + c2[g] * qs_[1 - k][g]
                flux = acc + oth if k == 0 else acc - oth
                store(f, k, jnp.where(alive, base[k][f] - mk[k] * flux, 0.0))

    def first_pass(i, sums):
        vb, t = i // 8, lax.rem(i, 8)
        v, b = vb // 2, lax.rem(vb, 2)
        r0 = t * 8
        row = iota8 + r0
        inner = jnp.logical_and(row > 0, row != rows[b] - 1)
        box = [jnp.zeros((8, 128), F32)]

        def store(f, k, val):
            fi[v, b, f, k, pl.ds(pl.multiple_of(r0 + 8, 8), 8), :] = val
            box[0] = box[0] + val * val

        advance_tile(st, v, b, t, 1.0, store)
        sq = jnp.where(inner, box[0], 0.0)
        s0, s1 = sums
        return s0 + jnp.where(v == 0, sq, 0.0), s1 + jnp.where(v == 1, sq, 0.0)

    ssq = lax.fori_loop(0, 32, first_pass, (zero8, zero8))

    def faces(i, _):
        b, side, v = i // 4, lax.rem(i // 2, 2), lax.rem(i, 2)
        last = jnp.maximum(rows[b] - 1, 1)
        r = jnp.where(side == 0, 0, last)
        adj = jnp.where(side == 0, 1, last - 1)
        slot = b * 2 + side
        lane_row = b * 8 + side * 2 + v
        for f in range(NF):
            for k in range(2):
                a = st[v, b, f, k, pl.ds(r + 8, 1), :]
                p = fi[v, b, f, k, pl.ds(r + 8, 1), :]
                pay[v, slot, f * 2 + k:f * 2 + k + 1, :] = a
                pay[v, slot, 10 + f * 2 + k:11 + f * 2 + k, :] = p
                own[f, pl.ds(lane_row + 4 * k, 1), :] = a
                own[NF + f, pl.ds(lane_row + 4 * k, 1), :] = p
        for k in range(2):
            m = met[b, k, pl.ds(r, 1), :]
            pay[v, slot, 20 + k:21 + k, :] = m
            pay[v, slot, 22 + k:23 + k, :] = m
            own[10, pl.ds(lane_row + 4 * k, 1), :] = m
            own[11, pl.ds(lane_row + 4 * k, 1), :] = met[b, k, pl.ds(adj, 1), :]
        return 0

    lax.fori_loop(0, 8, faces, 0)
    req = jnp.where(lane8 == 0, nbr[0, 0], jnp.where(lane8 == 1, nbr[0, 1], jnp.where(lane8 == 2, nbr[1, 0], nbr[1, 1])))
    rq[rho] = req

    pl.semaphore_wait(bar, n_part)

    mine = pltpu.make_async_copy(pay.at[c], zb.at[z, c], loc_sem.at[0])
    mine.start()
    z_copies = []
    for j in range(2):
        core = lax.rem(c + j, NC)
        for side, dz in ((0, 1), (1, -1)):
            n = side * 2 + j
            cp = rcopy(pay.at[core], zb.at[z, c], zs.at[n], zr.at[n], zdev(dz, core), x)
            cp.start()
            z_copies.append(cp)
    other = rcopy(pay.at[1 - c], zb.at[z, c], zs.at[4], zr.at[4], zdev(0, 1 - c), x)
    other.start()
    q_copies = []
    for d in range(1, NR):
        cp = rcopy(rq.at[rho], rq.at[rho], qs.at[d - 1], qr.at[d - 1], z * NR + lax.rem(rho + d, NR), x)
        cp.start()
        q_copies.append(cp)

    def second_pass(v):
        def body(i, _):
            b, t = i // 8, lax.rem(i, 8)

            def store(f, k, val):
                se[b * 2 + k, v, f, pl.ds(pl.multiple_of(t * 8, 8), 8), :] = val

            advance_tile(fi, v, b, t, SCALE, store)
            return 0

        lax.fori_loop(0, 16, body, 0)

    def xdev(d):
        return lax.rem(x + d + NX, NX)

    sends = []

    def send_second(v):
        far = xdev(2)
        for s, d in ((0, 1), (1, -1)):
            half = pl.ds(32 * s, 32)
            cp = rcopy(se.at[far, v, :, half, :], rel1.at[v, s], xs.at[v, s], xr.at[v, s], blk, xdev(d))
            cp.start()
            sends.append(cp)
        for s, d in ((0, 1), (1, -1)):
            cp = rcopy(se.at[xdev(d), v], gath.at[2 * x + v], xs.at[v, 2 + s], xr.at[v, 2 + s], blk, xdev(d))
            cp.start()
            sends.append(cp)

    def relay_second(v):
        cps = []
        for s, d in ((0, 1), (1, -1)):
            half = pl.ds(32 * s, 32)
            sends[v * 4 + s].wait_recv()
            src = xdev(-d)
            cp = rcopy(rel1.at[v, s], gath.at[2 * src + v, :, half, :], fs.at[v, s], fr.at[v, s], blk, xdev(d))
            cp.start()
            cps.append(cp)
        return cps

    second_pass(0)
    send_second(0)

    mine.wait()
    other.wait()
    for cp in z_copies:
        cp.wait()
    ring = []

    def ring_step(s):
        cps = []
        for side, dz in ((0, 1), (1, -1)):
            n = 5 + (s - 1) * 2 + side
            slot = lax.rem(z - dz * s + NZ, NZ)
            if s < 3:
                part = zb.at[slot]
            else:
                part = zb.at[slot, side]
            cp = rcopy(part, part, zs.at[n], zr.at[n], zdev(dz, c), x)
            cp.start()
            cps.append(cp)
        return cps

    ring1 = ring_step(1)
    second_pass(1)
    send_second(1)
    for cp in ring1:
        cp.wait()
    ring2 = ring_step(2)
    relays0 = relay_second(0)
    for cp in ring2:
        cp.wait()
    ring3 = ring_step(3)
    for cp in q_copies:
        cp.wait()
    tosmem = pltpu.make_async_copy(rq, rqs, loc_sem.at[1])
    tosmem.start()
    mygath = pltpu.make_async_copy(se.at[x], gath.at[pl.ds(2 * x, 2)], loc_sem.at[2])
    mygath.start()
    relays1 = relay_second(1)
    tosmem.wait()
    for cp in ring3:
        cp.wait()

    def pick(i, _):
        to, r = i // 4, lax.rem(i, 4)
        bid = rqs[to, 0, r]
        side = lax.rem(r, 2)
        o2[to, r] = zb[bid >> 4, (bid >> 1) & 1, (bid & 1) * 2 + (1 - side)]
        return 0

    lax.fori_loop(0, 4 * NR, pick, 0)
    y_copies = []
    for d in range(1, NR):
        to = lax.rem(rho + d, NR)
        cp = rcopy(o2.at[to], rb.at[rho], ys.at[d - 1], yr.at[d - 1], z * NR + to, x)
        cp.start()
        y_copies.append(cp)
    rb[rho] = o2[rho]
    for cp in y_copies:
        cp.wait()

    rev = 127 - lane8

    def unpack(i, _):
        b, side, v = i // 4, lax.rem(i // 2, 2), lax.rem(i, 2)
        r = b * 2 + side
        bid = nbr[b, side]
        f_ = flip[b, side]
        lane_row = b * 8 + side * 2 + v
        src = ((bid >> 2) & 3) * 2 + v
        for h in range(3):
            q = rb[src, r, 8 * h:8 * h + 8, :]
            turned = jnp.take_along_axis(q, rev, axis=1)
            rowh = iota8 + 8 * h
            neg = jnp.logical_or(jnp.logical_or(rowh == 2, rowh == 3), jnp.logical_or(rowh == 12, rowh == 13))
            turned = jnp.where(neg, -turned, turned)
            q = jnp.where(f_ > 0, turned, q)
            for j in range(8):
                w = 8 * h + j
                if w >= 22:
                    continue
                item, k = (w // 2, w % 2)
                gst[item, pl.ds(lane_row + 4 * k, 1), :] = q[j:j + 1, :]
        sign = jnp.where(f_ > 0, -1.0, 1.0) + jnp.zeros((1, 128), F32)
        for k in range(2):
            gst[11, pl.ds(lane_row + 4 * k, 1), :] = sign
        return 0

    lax.fori_loop(0, 8, unpack, 0)

    sig = jnp.where((iota8 >> 1) & 1 == 0, -1.0, 1.0)
    sk = jnp.where(iota8 < 4, 1.0, -1.0)
    odd = iota8 & 1

    def jmul(d, g_, f):
        acc = jac[d, f, 0] * g_[0]
        for g in range(1, NF):
            acc = acc + jac[d, f, g] * g_[g]
        return acc

    def fix(b, sums):
        base = pl.ds(pl.multiple_of(b * 8, 8), 8)
        g0 = [gst[f, base, :] for f in range(NF)]
        gf = [gst[NF + f, base, :] for f in range(NF)]
        gm = gst[10, base, :]
        turn = gst[11, base, :]
        o = [own[f, base, :] for f in range(NF)]
        of = [own[NF + f, base, :] for f in range(NF)]
        m0 = own[10, base, :]
        m1 = own[11, base, :]
        od = [o[f] * turn if f == 1 else o[f] for f in range(NF)]
        g1, c1 = [], []
        total = zero8
        for f in range(NF):
            tf = jmul(1, od, f)
            if f == 1:
                tf = tf * turn
            g1.append(gf[f] + VISC * o[f] + sig * gm * tf)
            cf = VISC * g0[f] - sig * m0 * jmul(1, g0, f)
            c1.append(cf)
            ff = of[f] + cf
            total = total + ff * ff
        e = [pltpu.roll(cf, 127, 1) for cf in c1]
        w = [pltpu.roll(cf, 1, 1) for cf in c1]
        ok = [pltpu.roll(cf, 4, 0) for cf in c1]
        ew = [a - b_ for a, b_ in zip(e, w)]
        for f in range(NF):
            flux = jmul(0, ew, f) + sk * jmul(2, ok, f) + sig * jmul(1, g1, f)
            face = (1.0 - 6.0 * VISC) * c1[f] + VISC * (e[f] + w[f] + ok[f] + g1[f]) - m0 * flux
            near = VISC * c1[f] - sig * m1 * jmul(1, c1, f)
            face = face * SCALE
            near = near * SCALE
            cs[b * 2, f, 0:4, :] = face[0:4]
            cs[b * 2, f, 4:8, :] = near[0:4]
            cs[b * 2 + 1, f, 0:4, :] = face[4:8]
            cs[b * 2 + 1, f, 4:8, :] = near[4:8]
        s0, s1 = sums
        return s0 + jnp.where(odd == 0, total, 0.0), s1 + jnp.where(odd == 1, total, 0.0)

    ssq = lax.fori_loop(0, 2, fix, ssq)
    c_copies = []
    for d in (2, 1, 3):
        cp = rcopy(cs.at[xdev(d)], cb.at[x], cs_s.at[d - 1], cs_r.at[d - 1], blk, xdev(d))
        cp.start()
        c_copies.append(cp)
    cb[x] = cs[x]

    mygath.wait()
    for cp in sends[2:4] + sends[6:8]:
        cp.wait()
    for cp in sends[0:2] + sends[4:6]:
        cp.wait_send()
    for cp in relays0 + relays1:
        cp.wait()
    for cp in c_copies:
        cp.wait()

    bq = x // 2
    my_last = jnp.where(bq == 0, rows[0], rows[1]) - 1

    def gram_tile(i, acc):
        f, t = i // 8, lax.rem(i, 8)
        row = iota8 + t * 8
        at = [row == 0, row == my_last, row == 1, row == my_last - 1]
        vals = []
        for v in range(8):
            q = gath[v, f, pl.ds(pl.multiple_of(t * 8, 8), 8), :]
            for n, (typ, side) in enumerate(((0, 0), (0, 1), (1, 0), (1, 1))):
                w = typ * 4 + side * 2 + v % 2
                q = q + jnp.where(at[n], jnp.broadcast_to(cb[v // 2, f, w:w + 1, :], (8, 128)), 0.0)
            gath[v, f, pl.ds(pl.multiple_of(t * 8, 8), 8), :] = q
            vals.append(q)
        res = list(acc)
        for v in range(8):
            for w in range(v + 1):
                res[pair(v, w)] = res[pair(v, w)] + vals[v] * vals[w]
        return tuple(res)

    grams = lax.fori_loop(0, 40, gram_tile, tuple(zero8 for _ in range(36)))
    gacc[...] = jnp.zeros((128, 128), F32)
    for n in range(36):
        gacc[n:n + 1, :] = jnp.sum(grams[n], axis=0, keepdims=True)
    for v in range(2):
        gacc[pl.ds(36 + 2 * x + v, 1), :] = jnp.sum(ssq[v], axis=0, keepdims=True)
    ones8 = jnp.ones((8, 128), F32)
    ar[...] = lax.dot_general(ones8, gacc[...], (((1,), (1,)), ((), ())), precision=HI, preferred_element_type=F32)

    def exchange(buf, me, n, first, dev):
        buf[me] = ar[...]
        cps = []
        for d in range(1, n):
            b_, x_ = dev(d)
            cp = rcopy(ar, buf.at[me], as_s.at[first + d - 1], as_r.at[first + d - 1], b_, x_)
            cp.start()
            cps.append(cp)
        for cp in cps:
            cp.wait()
        tot = buf[0]
        for j in range(1, n):
            tot = tot + buf[j]
        ar[...] = tot

    exchange(arx, x, NX, 0, lambda d: (blk, xdev(d)))
    exchange(ary, rho, NR, 3, lambda d: (z * NR + lax.rem(rho + d, NR), x))
    exchange(arz, z, NZ, 10, lambda d: (zdev(d, c), x))

    r48 = lax.broadcasted_iota(jnp.int32, (48, 128), 0)
    l48 = lax.broadcasted_iota(jnp.int32, (48, 128), 1)
    spread = jnp.where(r48 == l48, jnp.broadcast_to(ar[0:1, :], (48, 128)), 0.0)
    spl[...] = jnp.dot(spread, jnp.ones((128, 128), F32), precision=HI, preferred_element_type=F32)

    def entry(n):
        return spl[n:n + 1, :]

    s = [1.0 / (SCALE * jnp.sqrt(entry(36 + v) + EPS)) for v in range(8)]
    low = {}
    inv = []
    for j in range(8):
        a = entry(pair(j, j)) * s[j] * s[j]
        for k in range(j):
            a = a - low[j, k] * low[j, k]
        low[j, j] = jnp.sqrt(a)
        inv.append(1.0 / low[j, j])
        for i in range(j + 1, 8):
            a = entry(pair(i, j)) * s[i] * s[j]
            for k in range(j):
                a = a - low[i, k] * low[j, k]
            low[i, j] = a * inv[j]
    xx = {}
    for j in range(8):
        xx[j, j] = inv[j]
        for i in range(j + 1, 8):
            a = low[i, j] * xx[j, j]
            for k in range(j + 1, i):
                a = a + low[i, k] * xx[k, j]
            xx[i, j] = -a * inv[i]
    upper = zero8
    for i in range(8):
        for j in range(i + 1):
            mix[pair(i, j)] = jnp.broadcast_to(xx[i, j] * s[j], (8, 128))
            upper = jnp.where(jnp.logical_and(iota8 == j, lane8 == i), jnp.broadcast_to(low[i, j], (8, 128)), upper)
    fac[...] = upper[:, 0:8]

    def combine(i, _):
        f, t = i // 8, lax.rem(i, 8)
        rr = pl.ds(pl.multiple_of(t * 8, 8), 8)
        vals = [gath[v, f, rr, :] for v in range(8)]
        for v in range(8):
            a = mix[pair(v, 0)] * vals[0]
            for w in range(1, v + 1):
                a = a + mix[pair(v, w)] * vals[w]
            bas[v, f, rr, :] = a
        return 0

    lax.fori_loop(0, 40, combine, 0)
    kq = lax.rem(x, 2)
    homes, first_hops, relays = [], [], []
    far = xdev(2)
    for v in range(2):
        for sd, d in ((0, 1), (1, -1)):
            half = pl.ds(32 * sd, 32)
            cp = rcopy(bas.at[2 * far + v, :, half, :], rel2.at[v, sd], os.at[v, sd], orr.at[v, sd], blk, xdev(d))
            cp.start()
            first_hops.append(cp)
    for v in range(2):
        for sd, d in ((0, 1), (1, -1)):
            cp = rcopy(bas.at[2 * xdev(d) + v], out.at[v, bq, :, kq], os.at[v, 2 + sd], orr.at[v, 2 + sd], blk, xdev(d))
            cp.start()
            homes.append(cp)
    keep = []
    for v in range(2):
        cp = pltpu.make_async_copy(bas.at[2 * x + v], out.at[v, bq, :, kq], loc_sem.at[3 + v])
        cp.start()
        keep.append(cp)
    for v in range(2):
        for sd, d in ((0, 1), (1, -1)):
            half = pl.ds(32 * sd, 32)
            first_hops[v * 2 + sd].wait_recv()
            src = xdev(-d)
            cp = rcopy(rel2.at[v, sd], out.at[v, src // 2, :, lax.rem(src, 2), half, :], os.at[v, 4 + sd], orr.at[v, 4 + sd], blk, xdev(d))
            cp.start()
            relays.append(cp)
    for cp in keep:
        cp.wait()
    for cp in first_hops:
        cp.wait_send()
    for cp in homes + relays:
        cp.wait()


def per_device(vectors, metric, jacobians, block_rows, neighbours, flipped):
    vm = pl.BlockSpec(memory_space=pltpu.VMEM)
    sm = pl.BlockSpec(memory_space=pltpu.SMEM)
    dma = pltpu.SemaphoreType.DMA
    return pl.pallas_call(
        kernel,
        out_shape=(jax.ShapeDtypeStruct(vectors.shape, F32), jax.ShapeDtypeStruct((8, 8), F32)),
        in_specs=[vm, vm, sm, sm, sm, sm],
        out_specs=(pl.BlockSpec(memory_space=pl.ANY), vm),
        scratch_shapes=[
            pltpu.VMEM((2, 2, NF, 2, 80, 128), F32),
            pltpu.VMEM((2, 2, NF, 2, 80, 128), F32),
            pltpu.VMEM((4, 2, NF, 64, 128), F32),
            pltpu.VMEM((8, NF, 64, 128), F32),
            pltpu.VMEM((8, NF, 64, 128), F32),
            pltpu.VMEM((2, 2, NF, 32, 128), F32),
            pltpu.VMEM((2, 2, NF, 32, 128), F32),
            pltpu.VMEM((2, 4, 24, 128), F32),
            pltpu.VMEM((NZ, NC, 4, 24, 128), F32),
            pltpu.VMEM((NR, 8, 128), jnp.int32),
            pltpu.SMEM((NR, 8, 128), jnp.int32),
            pltpu.VMEM((NR, 4, 24, 128), F32),
            pltpu.VMEM((NR, 4, 24, 128), F32),
            pltpu.VMEM((12, 16, 128), F32),
            pltpu.VMEM((12, 16, 128), F32),
            pltpu.VMEM((4, NF, 8, 128), F32),
            pltpu.VMEM((4, NF, 8, 128), F32),
            pltpu.VMEM((128, 128), F32),
            pltpu.VMEM((8, 128), F32),
            pltpu.VMEM((NX, 8, 128), F32),
            pltpu.VMEM((NR, 8, 128), F32),
            pltpu.VMEM((NZ, 8, 128), F32),
            pltpu.VMEM((48, 128), F32),
            pltpu.VMEM((36, 8, 128), F32),
            dma((5,)),
            dma((2, 4)), dma((2, 4)),
            dma((2, 2)), dma((2, 2)),
            dma((11,)), dma((11,)),
            dma((7,)), dma((7,)),
            dma((7,)), dma((7,)),
            dma((3,)), dma((3,)),
            dma((17,)), dma((17,)),
            dma((2, 6)), dma((2, 6)),
        ],
        compiler_params=pltpu.CompilerParams(collective_id=0, has_side_effects=True, vmem_limit_bytes=48 * 1024 * 1024),
        cost_estimate=pl.CostEstimate(flops=60_000_000, bytes_accessed=4_000_000, transcendentals=0),
    )(vectors, metric, jacobians, block_rows, neighbours, flipped)


def solution(mesh):
    wide = P("vec", "blk", None, None, None, None)
    in_specs = (wide, P("blk", None, None, None), P(), P("blk"), P("blk", None), P("blk", None))
    return jax.shard_map(per_device, mesh=mesh, in_specs=in_specs, out_specs=(wide, P()), check_vma=False)
```

time: 645 us -> 79.1 us (0.12); the launches traced: 633 us -> 77.7 us
  blocking collectives: 202 us -> 0 us
  waiting for transfers between devices: 186 us -> 0 us
  local copies, waits for them, and re-layouts: 157 us -> 6.59 us
  Pallas kernels: 0 us -> 70.5 us
  matrix products: 58.5 us -> 0 us
  other arithmetic: 13.9 us -> 0 us
  between operations: 14.5 us -> 0.64 us
    psum x2 -> x0, blocking collectives: 202 us -> none  [the longest x1 127 us: per_device(): vector_norms = jnp.sqrt(lax.psum(own_squares, 'blk') + epsilon)]
    all_gather x3 -> x0, waiting for transfers between devices: 186 us -> none  [the longest x2 130 us: advance(): everyone = lax.all_gather(faces, 'blk', axis=1, tiled=True)]
    gather x7 -> x0, local copies, waits for them, and re-layouts: 121 us -> none  [the longest x3 111 us: block_faces(): jnp.take_along_axis(field_state, jnp.broadcast_to(last_index, full_shape)...]
    pallas_call x0 -> x1, Pallas kernels: none -> 70.5 us  [per_device(): pl.pallas_call(kernel, out_shape=(jax.ShapeDtypeStruct(vectors.shape, F32...]
    dot_general x8 -> x0, matrix products: 58.3 us -> none  [the longest x2 21 us: local_update(): jnp.einsum('fg,vbgkji->vbfkji', jacobians[1], above_cells - below_cells,...]
    all_gather x2 -> x0, local copies, waits for them, and re-layouts: 10.2 us -> none  [advance(): everyone = lax.all_gather(faces, 'blk', axis=1, tiled=True)]
    unnamed x65 -> x13, local copies, waits for them, and re-layouts: 16.4 us -> 6.59 us
    slice x10 -> x0, local copies, waits for them, and re-layouts: 7.85 us -> none  [the longest x2 4.67 us: local_update(): field_state[:, :, :, :, 1:, :]]
  transfers between devices with their start and end apart: 3 -> 0, of which waited for: 3 -> 0; matrix products, arithmetic and copies ran while one was open for 4% -> 0% of each run, Pallas kernels for 0% -> 0%
where the time goes in v1:
time: 79.1 us; the launch traced here: 77.7 us
  Pallas kernels  70.5 us (89%)
  local copies, waits for them, and re-layouts  6.59 us (8%)
    pallas_call x1, Pallas kernels, per_device(): pl.pallas_call(kernel, out_shape=(jax.ShapeDtypeStruct(vectors.shape, F32...  70.5 us
    unnamed x13, local copies, waits for them, and re-layouts  6.59 us

profile of v1, /device:TPU:4, one launch (start us, length us, event | category | flops | bytes accessed | tf_op | source)
XLA Modules:
  0.0 77.7 jit_solution(13768065818725992150)
XLA Ops:
  0.6 0.7 copy.8.jac
  1.3 0.0 copy-start
  1.3 1.3 %copy-done = f32[2,2,5,2,64,128]{5,4,3,2,1,0:T(8,128)S(1)} copy-done((f32[2,2,5,2,64,128]{5,4,3,2,1,0:T(8,128)S(1)}, f32[2,2,5,2,64,128]{5,4,3,2,1,0:T(8,128)}, u32[]{:S(2)}) %copy-start) | copy-done | bytes 1310744
  2.7 0.0 copy-start.1
  2.7 0.9 %copy-done.1 = f32[2,2,64,128]{3,2,1,0:T(8,128)S(1)} copy-done((f32[2,2,64,128]{3,2,1,0:T(8,128)S(1)}, f32[2,2,64,128]{3,2,1,0:T(8,128)}, u32[]{:S(2)}) %copy-start.1) | copy-done | bytes 131096
  3.6 0.0 copy-start.2
  3.6 0.7 copy-done.2
  4.2 0.0 copy-start.3
  4.2 0.7 copy-done.3
  4.9 0.0 copy-start.4
  4.9 0.7 copy-done.4
  5.6 70.5 %shard_map.77 = (f32[2,2,5,2,64,128]{5,4,3,2,1,0:T(8,128)S(1)}, f32[8,8]{1,0:T(8,128)S(1)}) custom-call(f32[2,2,5,2,64,128]{5,4,3,2,1,0:T(8,128)S(1)} %copy-done, f32[2,2,64,128]{3,2,1,0:T(8,128)S(1)} %copy-done.1, f32[3,5,5]{2,1,0:T(8,128)S(1)} %copy.8.jac, s32[2]{0:T(128)S(1)} %copy-done.4, s32[2,2]{1,0:T(2,128)S(1)} %copy-done.2, s32[2,2]{1,0:T(2,128)S(1)} %copy-done.3), custom_call_target="tpu_custom_call" | custom-call | flops 60000000 | bytes 4000000 | tf_op jit(solution)/shard_map/pallas_call | solution.py:512
  76.0 1.1 %copy.11 = f32[2,2,5,2,64,128]{5,4,3,2,1,0:T(8,128)} copy(f32[2,2,5,2,64,128]{5,4,3,2,1,0:T(8,128)S(1)} %get-tuple-element.4) | data formatting | bytes 2621440
  77.1 0.6 copy.12
Async XLA Ops:
  1.3 1.3 %copy-start = (f32[2,2,5,2,64,128]{5,4,3,2,1,0:T(8,128)S(1)}, f32[2,2,5,2,64,128]{5,4,3,2,1,0:T(8,128)}, u32[]{:S(2)}) copy-start(f32[2,2,5,2,64,128]{5,4,3,2,1,0:T(8,128)} %vec.1) | copy-start | bytes 3932164
  2.7 0.9 %copy-start.1 = (f32[2,2,64,128]{3,2,1,0:T(8,128)S(1)}, f32[2,2,64,128]{3,2,1,0:T(8,128)}, u32[]{:S(2)}) copy-start(f32[2,2,64,128]{3,2,1,0:T(8,128)} %met.1) | copy-start | bytes 393220
  3.6 0.7 copy-start.2
  4.2 0.7 copy-start.3
  4.9 0.7 copy-start.4

commit v2 on v1

--- a/solution.py
+++ b/solution.py
@@ -20,9 +20,9 @@
     return v * (v + 1) // 2 + w
 
 
-def kernel(vec, met, jac, rows, nbr, flip, out, fac,
-           st, fi, se, gath, bas, rel1, rel2, pay, zb, rq, rqs, o2, rb, own, gst, cs, cb, gacc, ar, arx, ary, arz, spl, mix,
-           loc_sem, xs, xr, fs, fr, zs, zr, qs, qr, ys, yr, cs_s, cs_r, as_s, as_r, os, orr):
+def kernel(vec_h, met_h, jac_h, rows_h, nbr_h, flip_h, out, fac,
+           vec, met, jac, rows, nbr, flip, st, fi, se, gath, bas, pay, zb, rq, rqs, o2, rb, own, gst, cs, cb, gacc, ar, ar2, arx, ary, spl, mix,
+           loc_sem, in_sem, vec_sem, xs, xr, zs, zr, qs, qr, ys, yr, cs_s, cs_r, as_s, as_r, os, orr):
     blk = lax.axis_index("blk")
     x = lax.axis_index("vec")
     z = blk // NR
@@ -34,20 +34,32 @@
         zz = lax.rem(z + dz + NZ, NZ)
         return zz * NR + (rho - c) + core
 
+    small = [pltpu.make_async_copy(h, d, in_sem.at[n]) for n, (h, d) in enumerate(
+        ((rows_h, rows), (jac_h, jac), (nbr_h, nbr), (flip_h, flip), (met_h, met)))]
+    big = [pltpu.make_async_copy(vec_h.at[n // 2, n % 2], vec.at[n // 2, n % 2], vec_sem.at[n]) for n in range(4)]
+    for cp in small[:1] + big + small[1:]:
+        cp.start()
+
     bar = pltpu.get_barrier_semaphore()
-    n_part = 0
-    for d in range(1, NX):
-        pl.semaphore_signal(bar, inc=1, device_id={"blk": blk, "vec": lax.rem(x + d, NX)}, device_id_type=MESH)
-        n_part += 1
-    for d in range(1, NR):
-        pl.semaphore_signal(bar, inc=1, device_id={"blk": z * NR + lax.rem(rho + d, NR), "vec": x}, device_id_type=MESH)
-        n_part += 1
-    for d in range(1, NZ):
-        pl.semaphore_signal(bar, inc=1, device_id={"blk": zdev(d, c), "vec": x}, device_id_type=MESH)
-        n_part += 1
-    for d in (1, NZ - 1):
-        pl.semaphore_signal(bar, inc=1, device_id={"blk": zdev(d, 1 - c), "vec": x}, device_id_type=MESH)
-        n_part += 1
+    def xdev(d):
+        return lax.rem(x + d + NX, NX)
+
+    def zc(d):
+        m = lax.rem(z * NC + c + d, NZ * NC)
+        return (m // NC) * NR + (rho - c) + lax.rem(m, NC), x
+
+    def yx(d):
+        m = lax.rem((rho // NC) * NX + x + d, (NR // NC) * NX)
+        return z * NR + (m // NX) * NC + c, lax.rem(m, NX)
+
+    def yc(d):
+        return z * NR + lax.rem(rho + d, NR), x
+
+    partners = [zc(d) for d in range(1, 16)] + [yx(d) for d in range(1, 16)]
+    partners += [(z * NR + lax.rem(rho - c + NC * d, NR) + 1 - c, x) for d in range(1, NR // NC)]
+    for b_, x_ in partners:
+        pl.semaphore_signal(bar, inc=1, device_id={"blk": b_, "vec": x_}, device_id_type=MESH)
+    n_part = len(partners)
 
     def rcopy(src, dst, ssem, rsem, b_, x_):
         return pltpu.make_async_remote_copy(src_ref=src, dst_ref=dst, send_sem=ssem, recv_sem=rsem,
@@ -71,7 +83,12 @@
         fi[v, b, f, k, 72:80, :] = zero8
         return 0
 
-    lax.fori_loop(0, 40, fill, 0)
+    small[0].wait()
+    for n in range(4):
+        big[n].wait()
+        lax.fori_loop(10 * n, 10 * n + 10, fill, 0)
+    for cp in small[1:]:
+        cp.wait()
 
     def advance_tile(src, v, b, t, scale, store):
         r0 = pl.multiple_of(t * 8, 8)
@@ -96,9 +113,9 @@
             base.append(ab)
         mk = [met[b, k, pl.ds(r0, 8), :] * scale for k in range(2)]
         for f in range(NF):
-            c0 = [jac[0, f, g] for g in range(NF)]
-            c1 = [jac[1, f, g] for g in range(NF)]
-            c2 = [jac[2, f, g] for g in range(NF)]
+            c0 = [jac[f, 0, g] for g in range(NF)]
+            c1 = [jac[f, 1, g] for g in range(NF)]
+            c2 = [jac[f, 2, g] for g in range(NF)]
             for k in range(2):
                 acc = c0[0] * d0[k][0] + c1[0] * d1[k][0]
                 oth = c2[0] * qs_[1 - k][0]
@@ -162,7 +179,7 @@
     for j in range(2):
         core = lax.rem(c + j, NC)
         for side, dz in ((0, 1), (1, -1)):
-            n = side * 2 + j
+            n = j * 2 + side
             cp = rcopy(pay.at[core], zb.at[z, c], zs.at[n], zr.at[n], zdev(dz, core), x)
             cp.start()
             z_copies.append(cp)
@@ -186,77 +203,53 @@
 
         lax.fori_loop(0, 16, body, 0)
 
-    def xdev(d):
-        return lax.rem(x + d + NX, NX)
-
     sends = []
 
     def send_second(v):
-        far = xdev(2)
-        for s, d in ((0, 1), (1, -1)):
-            half = pl.ds(32 * s, 32)
-            cp = rcopy(se.at[far, v, :, half, :], rel1.at[v, s], xs.at[v, s], xr.at[v, s], blk, xdev(d))
+        for d in (2, 1, 3):
+            cp = rcopy(se.at[xdev(d), v], gath.at[2 * x + v], xs.at[v, d - 1], xr.at[v, d - 1], blk, xdev(d))
             cp.start()
             sends.append(cp)
-        for s, d in ((0, 1), (1, -1)):
-            cp = rcopy(se.at[xdev(d), v], gath.at[2 * x + v], xs.at[v, 2 + s], xr.at[v, 2 + s], blk, xdev(d))
-            cp.start()
-            sends.append(cp)
-
-    def relay_second(v):
-        cps = []
-        for s, d in ((0, 1), (1, -1)):
-            half = pl.ds(32 * s, 32)
-            sends[v * 4 + s].wait_recv()
-            src = xdev(-d)
-            cp = rcopy(rel1.at[v, s], gath.at[2 * src + v, :, half, :], fs.at[v, s], fr.at[v, s], blk, xdev(d))
-            cp.start()
-            cps.append(cp)
-        return cps
 
     second_pass(0)
     send_second(0)
 
-    mine.wait()
-    other.wait()
-    for cp in z_copies:
-        cp.wait()
-    ring = []
-
-    def ring_step(s):
+    drain = z_copies + [other]
+
+    def ring_step(s, before):
         cps = []
-        for side, dz in ((0, 1), (1, -1)):
-            n = 5 + (s - 1) * 2 + side
-            slot = lax.rem(z - dz * s + NZ, NZ)
-            if s < 3:
-                part = zb.at[slot]
-            else:
-                part = zb.at[slot, side]
-            cp = rcopy(part, part, zs.at[n], zr.at[n], zdev(dz, c), x)
-            cp.start()
-            cps.append(cp)
+        for j in range(2):
+            core = lax.rem(c + j, NC)
+            for side, dz in ((0, 1), (1, -1)):
+                if s == 3 and side != j:
+                    before[j * 2 + side].wait_recv()
+                    continue
+                n = 5 + (s - 1) * 4 + j * 2 + side
+                slot = lax.rem(z - dz * s + NZ, NZ)
+                part = zb.at[slot, core]
+                before[j * 2 + side].wait_recv()
+                cp = rcopy(part, part, zs.at[n], zr.at[n], zdev(dz, c), x)
+                cp.start()
+                cps.append(cp)
+        drain.extend(cps)
         return cps
 
-    ring1 = ring_step(1)
+    ring1 = ring_step(1, z_copies)
     second_pass(1)
     send_second(1)
-    for cp in ring1:
-        cp.wait()
-    ring2 = ring_step(2)
-    relays0 = relay_second(0)
-    for cp in ring2:
-        cp.wait()
-    ring3 = ring_step(3)
+    ring2 = ring_step(2, ring1)
+    mygath = pltpu.make_async_copy(se.at[x], gath.at[pl.ds(2 * x, 2)], loc_sem.at[2])
+    mygath.start()
     for cp in q_copies:
-        cp.wait()
+        cp.wait_recv()
     tosmem = pltpu.make_async_copy(rq, rqs, loc_sem.at[1])
     tosmem.start()
-    mygath = pltpu.make_async_copy(se.at[x], gath.at[pl.ds(2 * x, 2)], loc_sem.at[2])
-    mygath.start()
-    relays1 = relay_second(1)
+    ring3 = ring_step(3, ring2)
+    mine.wait()
+    other.wait_recv()
     tosmem.wait()
     for cp in ring3:
-        cp.wait()
+        cp.wait_recv()
 
     def pick(i, _):
         to, r = i // 4, lax.rem(i, 4)
@@ -274,7 +267,8 @@
         y_copies.append(cp)
     rb[rho] = o2[rho]
     for cp in y_copies:
-        cp.wait()
+        cp.wait_recv()
+    drain += y_copies + q_copies
 
     rev = 127 - lane8
 
@@ -310,9 +304,9 @@
     odd = iota8 & 1
 
     def jmul(d, g_, f):
-        acc = jac[d, f, 0] * g_[0]
+        acc = jac[f, d, 0] * g_[0]
         for g in range(1, NF):
-            acc = acc + jac[d, f, g] * g_[g]
+            acc = acc + jac[f, d, g] * g_[g]
         return acc
 
     def fix(b, sums):
@@ -363,14 +357,9 @@
     cb[x] = cs[x]
 
     mygath.wait()
-    for cp in sends[2:4] + sends[6:8]:
-        cp.wait()
-    for cp in sends[0:2] + sends[4:6]:
-        cp.wait_send()
-    for cp in relays0 + relays1:
-        cp.wait()
-    for cp in c_copies:
-        cp.wait()
+    for cp in sends + c_copies:
+        cp.wait_recv()
+    drain += sends + c_copies
 
     bq = x // 2
     my_last = jnp.where(bq == 0, rows[0], rows[1]) - 1
@@ -402,28 +391,28 @@
     ones8 = jnp.ones((8, 128), F32)
     ar[...] = lax.dot_general(ones8, gacc[...], (((1,), (1,)), ((), ())), precision=HI, preferred_element_type=F32)
 
-    def exchange(buf, me, n, first, dev):
-        buf[me] = ar[...]
+    def exchange(src, buf, me, first, dev):
+        buf[me] = src[...]
         cps = []
-        for d in range(1, n):
+        for d in range(1, 16):
             b_, x_ = dev(d)
-            cp = rcopy(ar, buf.at[me], as_s.at[first + d - 1], as_r.at[first + d - 1], b_, x_)
+            cp = rcopy(src, buf.at[me], as_s.at[first + d - 1], as_r.at[first + d - 1], b_, x_)
             cp.start()
             cps.append(cp)
         for cp in cps:
-            cp.wait()
-        tot = buf[0]
-        for j in range(1, n):
-            tot = tot + buf[j]
-        ar[...] = tot
-
-    exchange(arx, x, NX, 0, lambda d: (blk, xdev(d)))
-    exchange(ary, rho, NR, 3, lambda d: (z * NR + lax.rem(rho + d, NR), x))
-    exchange(arz, z, NZ, 10, lambda d: (zdev(d, c), x))
+            cp.wait_recv()
+        drain.extend(cps)
+        tot = [buf[j] for j in range(16)]
+        while len(tot) > 1:
+            tot = [a + b_ for a, b_ in zip(tot[::2], tot[1::2])]
+        return tot[0]
+
+    ar2[...] = exchange(ar, arx, z * NC + c, 0, zc)
+    ar3 = exchange(ar2, ary, (rho // NC) * NX + x, 15, yx)
 
     r48 = lax.broadcasted_iota(jnp.int32, (48, 128), 0)
     l48 = lax.broadcasted_iota(jnp.int32, (48, 128), 1)
-    spread = jnp.where(r48 == l48, jnp.broadcast_to(ar[0:1, :], (48, 128)), 0.0)
+    spread = jnp.where(r48 == l48, jnp.broadcast_to(ar3[0:1, :], (48, 128)), 0.0)
     spl[...] = jnp.dot(spread, jnp.ones((128, 128), F32), precision=HI, preferred_element_type=F32)
 
     def entry(n):
@@ -436,8 +425,8 @@
         a = entry(pair(j, j)) * s[j] * s[j]
         for k in range(j):
             a = a - low[j, k] * low[j, k]
-        low[j, j] = jnp.sqrt(a)
-        inv.append(1.0 / low[j, j])
+        inv.append(lax.rsqrt(a))
+        low[j, j] = a * inv[j]
         for i in range(j + 1, 8):
             a = entry(pair(i, j)) * s[i] * s[j]
             for k in range(j):
@@ -471,17 +460,10 @@
 
     lax.fori_loop(0, 40, combine, 0)
     kq = lax.rem(x, 2)
-    homes, first_hops, relays = [], [], []
-    far = xdev(2)
+    homes = []
     for v in range(2):
-        for sd, d in ((0, 1), (1, -1)):
-            half = pl.ds(32 * sd, 32)
-            cp = rcopy(bas.at[2 * far + v, :, half, :], rel2.at[v, sd], os.at[v, sd], orr.at[v, sd], blk, xdev(d))
-            cp.start()
-            first_hops.append(cp)
-    for v in range(2):
-        for sd, d in ((0, 1), (1, -1)):
-            cp = rcopy(bas.at[2 * xdev(d) + v], out.at[v, bq, :, kq], os.at[v, 2 + sd], orr.at[v, 2 + sd], blk, xdev(d))
+        for d in (2, 1, 3):
+            cp = rcopy(bas.at[2 * xdev(d) + v], out.at[v, bq, :, kq], os.at[v, d - 1], orr.at[v, d - 1], blk, xdev(d))
             cp.start()
             homes.append(cp)
     keep = []
@@ -489,39 +471,35 @@
         cp = pltpu.make_async_copy(bas.at[2 * x + v], out.at[v, bq, :, kq], loc_sem.at[3 + v])
         cp.start()
         keep.append(cp)
-    for v in range(2):
-        for sd, d in ((0, 1), (1, -1)):
-            half = pl.ds(32 * sd, 32)
-            first_hops[v * 2 + sd].wait_recv()
-            src = xdev(-d)
-            cp = rcopy(rel2.at[v, sd], out.at[v, src // 2, :, lax.rem(src, 2), half, :], os.at[v, 4 + sd], orr.at[v, 4 + sd], blk, xdev(d))
-            cp.start()
-            relays.append(cp)
     for cp in keep:
         cp.wait()
-    for cp in first_hops:
+    for cp in drain:
         cp.wait_send()
-    for cp in homes + relays:
+    for cp in homes:
         cp.wait()
 
 
 def per_device(vectors, metric, jacobians, block_rows, neighbours, flipped):
     vm = pl.BlockSpec(memory_space=pltpu.VMEM)
-    sm = pl.BlockSpec(memory_space=pltpu.SMEM)
+    hbm = pl.BlockSpec(memory_space=pltpu.HBM)
     dma = pltpu.SemaphoreType.DMA
     return pl.pallas_call(
         kernel,
         out_shape=(jax.ShapeDtypeStruct(vectors.shape, F32), jax.ShapeDtypeStruct((8, 8), F32)),
-        in_specs=[vm, vm, sm, sm, sm, sm],
+        in_specs=[hbm] * 6,
         out_specs=(pl.BlockSpec(memory_space=pl.ANY), vm),
         scratch_shapes=[
+            pltpu.VMEM(vectors.shape, F32),
+            pltpu.VMEM(metric.shape, F32),
+            pltpu.SMEM((NF, 3, NF), F32),
+            pltpu.SMEM((2,), jnp.int32),
+            pltpu.SMEM((2, 2), jnp.int32),
+            pltpu.SMEM((2, 2), jnp.int32),
             pltpu.VMEM((2, 2, NF, 2, 80, 128), F32),
             pltpu.VMEM((2, 2, NF, 2, 80, 128), F32),
             pltpu.VMEM((4, 2, NF, 64, 128), F32),
             pltpu.VMEM((8, NF, 64, 128), F32),
             pltpu.VMEM((8, NF, 64, 128), F32),
-            pltpu.VMEM((2, 2, NF, 32, 128), F32),
-            pltpu.VMEM((2, 2, NF, 32, 128), F32),
             pltpu.VMEM((2, 4, 24, 128), F32),
             pltpu.VMEM((NZ, NC, 4, 24, 128), F32),
             pltpu.VMEM((NR, 8, 128), jnp.int32),
@@ -534,24 +512,23 @@
             pltpu.VMEM((4, NF, 8, 128), F32),
             pltpu.VMEM((128, 128), F32),
             pltpu.VMEM((8, 128), F32),
-            pltpu.VMEM((NX, 8, 128), F32),
-            pltpu.VMEM((NR, 8, 128), F32),
-            pltpu.VMEM((NZ, 8, 128), F32),
+            pltpu.VMEM((8, 128), F32),
+            pltpu.VMEM((16, 8, 128), F32),
+            pltpu.VMEM((16, 8, 128), F32),
             pltpu.VMEM((48, 128), F32),
             pltpu.VMEM((36, 8, 128), F32),
-            dma((5,)),
-            dma((2, 4)), dma((2, 4)),
-            dma((2, 2)), dma((2, 2)),
-            dma((11,)), dma((11,)),
+            dma((5,)), dma((5,)), dma((4,)),
+            dma((2, 3)), dma((2, 3)),
+            dma((17,)), dma((17,)),
             dma((7,)), dma((7,)),
             dma((7,)), dma((7,)),
             dma((3,)), dma((3,)),
-            dma((17,)), dma((17,)),
-            dma((2, 6)), dma((2, 6)),
+            dma((30,)), dma((30,)),
+            dma((2, 3)), dma((2, 3)),
         ],
-        compiler_params=pltpu.CompilerParams(collective_id=0, has_side_effects=True, vmem_limit_bytes=48 * 1024 * 1024),
+        compiler_params=pltpu.CompilerParams(collective_id=0, has_side_effects=True, vmem_limit_bytes=62 * 1024 * 1024),
         cost_estimate=pl.CostEstimate(flops=60_000_000, bytes_accessed=4_000_000, transcendentals=0),
-    )(vectors, metric, jacobians, block_rows, neighbours, flipped)
+    )(vectors, metric, jnp.transpose(jacobians, (1, 0, 2)), block_rows, neighbours, flipped)
 
 
 def solution(mesh):

time: 79.1 us -> 72 us (0.910)
  the two profiles are of different devices: /device:TPU:4 before, /device:TPU:1 now
where the time goes in v2:
time: 72 us; the launch traced here: 71.9 us
  Pallas kernels  68.1 us (95%)
  local copies, waits for them, and re-layouts  3.12 us (4%)
    pallas_call x1, Pallas kernels, per_device(): pl.pallas_call(kernel, out_shape=(jax.ShapeDtypeStruct(vectors.shape, F32...  68.1 us
    unnamed x4, local copies, waits for them, and re-layouts  3.12 us

profile of v2, /device:TPU:1, one launch (start us, length us, event | category | flops | bytes accessed | tf_op | source)
XLA Modules:
  0.0 71.9 jit_solution(10429215199369080524)
XLA Ops:
  0.6 68.1 %shard_map.77 = (f32[2,2,5,2,64,128]{5,4,3,2,1,0:T(8,128)}, f32[8,8]{1,0:T(8,128)}) custom-call(f32[2,2,5,2,64,128]{5,4,3,2,1,0:T(8,128)} %vec_h.1, f32[2,2,64,128]{3,2,1,0:T(8,128)} %met_h.1, f32[5,3,5]{2,1,0:T(4,128)} %bitcast.1, s32[2]{0:T(128)} %rows_h.1, s32[2,2]{1,0:T(2,128)} %nbr_h.1, s32[2,2]{1,0:T(2,128)} %flip_h.1), custom_call_target="tpu_custom_call" | custom-call | flops 60000000 | bytes 4000000 | tf_op jit(solution)/shard_map/pallas_call | solution.py:486
  68.7 0.0 copy-start
  68.7 2.5 %copy.10 = f32[2,2,5,2,64,128]{5,4,3,2,1,0:T(8,128)} copy(f32[2,2,5,2,64,128]{5,4,3,2,1,0:T(8,128)} %get-tuple-element.4) | data formatting | bytes 2621440
  71.3 0.0 copy-done
  71.3 0.6 copy.11
Async XLA Ops:
  68.7 2.5 %copy-start = (f32[8,8]{1,0:T(8,128)S(1)}, f32[8,8]{1,0:T(8,128)}, u32[]{:S(2)}) copy-start(f32[8,8]{1,0:T(8,128)} %get-tuple-element.5) | copy-start | bytes 772

commit v3 on v2

--- a/solution.py
+++ b/solution.py
@@ -16,13 +16,20 @@
 SCALE = 1024.0
 
 
+DIRECT = [(0, 0, 0, 3), (0, 0, 2, 1), (1, 1, 1, 3), (1, 1, 0, 2), (2, 2, 0, 3), (0, 0, 1, 3), (0, 0, 0, 1), (1, 1, 1, 2), (2, 2, 1, 3),
+          (0, 0, 2, 3), (0, 0, 3, 1), (1, 1, 3, 2), (2, 2, 2, 3)]
+PASSED = [(1, 0, 1, 2), (3, 0, 3, 2), (2, 1, 2, 3), (0, 1, 0, 3)]
+LATE = [(3, 0, 0, 2)]
+MOVES = DIRECT + PASSED + LATE
+
+
 def pair(v, w):
     return v * (v + 1) // 2 + w
 
 
 def kernel(vec_h, met_h, jac_h, rows_h, nbr_h, flip_h, out, fac,
-           vec, met, jac, rows, nbr, flip, st, fi, se, gath, bas, pay, zb, rq, rqs, o2, rb, own, gst, cs, cb, gacc, ar, ar2, arx, ary, spl, mix,
-           loc_sem, in_sem, vec_sem, xs, xr, zs, zr, qs, qr, ys, yr, cs_s, cs_r, as_s, as_r, os, orr):
+           vec, met, jac, rows, nbr, flip, st, fi, gath, bas, pay, zb, rq, rqs, o2, rb, own, gst, cb, cb2, gacc, ar, ar2, arx, ary, spl, mix,
+           loc_sem, in_sem, vec_sem, xs, xr, zs, zr, qs, qr, ys, yr, cs_s, cs_r, as_s, as_r, ws, wr, cs2_s, cs2_r, out_sem):
     blk = lax.axis_index("blk")
     x = lax.axis_index("vec")
     z = blk // NR
@@ -55,8 +62,8 @@
     def yc(d):
         return z * NR + lax.rem(rho + d, NR), x
 
-    partners = [zc(d) for d in range(1, 16)] + [yx(d) for d in range(1, 16)]
-    partners += [(z * NR + lax.rem(rho - c + NC * d, NR) + 1 - c, x) for d in range(1, NR // NC)]
+    partners = [(zdev(dz, core), x) for dz in (1, -1) for core in range(2)] + [yc(d) for d in range(1, NR)]
+    partners += [(blk, xdev(d)) for d in range(1, NX)]
     for b_, x_ in partners:
         pl.semaphore_signal(bar, inc=1, device_id={"blk": b_, "vec": x_}, device_id_type=MESH)
     n_part = len(partners)
@@ -196,7 +203,7 @@
             b, t = i // 8, lax.rem(i, 8)
 
             def store(f, k, val):
-                se[b * 2 + k, v, f, pl.ds(pl.multiple_of(t * 8, 8), 8), :] = val
+                gath[x, b * 2 + k, v, f, pl.ds(pl.multiple_of(t * 8, 8), 8), :] = val
 
             advance_tile(fi, v, b, t, SCALE, store)
             return 0
@@ -207,9 +214,22 @@
 
     def send_second(v):
         for d in (2, 1, 3):
-            cp = rcopy(se.at[xdev(d), v], gath.at[2 * x + v], xs.at[v, d - 1], xr.at[v, d - 1], blk, xdev(d))
+            here = gath.at[x, xdev(d), v]
+            cp = rcopy(here, here, xs.at[v, d - 1], xr.at[v, d - 1], blk, xdev(d))
             cp.start()
             sends.append(cp)
+
+    def move(n):
+        frm, src, q, to = MOVES[n]
+        part = gath.at[src, q]
+        return rcopy(part, part, ws.at[n], wr.at[n], blk, jnp.int32(to))
+
+    def moves(which):
+        for n in range(len(MOVES)):
+            if MOVES[n] in which:
+                @pl.when(x == MOVES[n][0])
+                def _():
+                    move(n).start()
 
     second_pass(0)
     send_second(0)
@@ -238,8 +258,6 @@
     second_pass(1)
     send_second(1)
     ring2 = ring_step(2, ring1)
-    mygath = pltpu.make_async_copy(se.at[x], gath.at[pl.ds(2 * x, 2)], loc_sem.at[2])
-    mygath.start()
     for cp in q_copies:
         cp.wait_recv()
     tosmem = pltpu.make_async_copy(rq, rqs, loc_sem.at[1])
@@ -266,6 +284,7 @@
         cp.start()
         y_copies.append(cp)
     rb[rho] = o2[rho]
+    moves(DIRECT)
     for cp in y_copies:
         cp.wait_recv()
     drain += y_copies + q_copies
@@ -341,23 +360,25 @@
             near = VISC * c1[f] - sig * m1 * jmul(1, c1, f)
             face = face * SCALE
             near = near * SCALE
-            cs[b * 2, f, 0:4, :] = face[0:4]
-            cs[b * 2, f, 4:8, :] = near[0:4]
-            cs[b * 2 + 1, f, 0:4, :] = face[4:8]
-            cs[b * 2 + 1, f, 4:8, :] = near[4:8]
+            cb[x, b * 2, f, 0:4, :] = face[0:4]
+            cb[x, b * 2, f, 4:8, :] = near[0:4]
+            cb[x, b * 2 + 1, f, 0:4, :] = face[4:8]
+            cb[x, b * 2 + 1, f, 4:8, :] = near[4:8]
         s0, s1 = sums
         return s0 + jnp.where(odd == 0, total, 0.0), s1 + jnp.where(odd == 1, total, 0.0)
 
     ssq = lax.fori_loop(0, 2, fix, ssq)
     c_copies = []
     for d in (2, 1, 3):
-        cp = rcopy(cs.at[xdev(d)], cb.at[x], cs_s.at[d - 1], cs_r.at[d - 1], blk, xdev(d))
+        here = cb.at[x, xdev(d)]
+        cp = rcopy(here, here, cs_s.at[d - 1], cs_r.at[d - 1], blk, xdev(d))
         cp.start()
         c_copies.append(cp)
-    cb[x] = cs[x]
-
-    mygath.wait()
-    for cp in sends + c_copies:
+    for cp in sends:
+        cp.wait_recv()
+    moves(PASSED)
+
+    for cp in c_copies:
         cp.wait_recv()
     drain += sends + c_copies
 
@@ -370,11 +391,10 @@
         at = [row == 0, row == my_last, row == 1, row == my_last - 1]
         vals = []
         for v in range(8):
-            q = gath[v, f, pl.ds(pl.multiple_of(t * 8, 8), 8), :]
+            q = gath[v // 2, x, v % 2, f, pl.ds(pl.multiple_of(t * 8, 8), 8), :]
             for n, (typ, side) in enumerate(((0, 0), (0, 1), (1, 0), (1, 1))):
                 w = typ * 4 + side * 2 + v % 2
-                q = q + jnp.where(at[n], jnp.broadcast_to(cb[v // 2, f, w:w + 1, :], (8, 128)), 0.0)
-            gath[v, f, pl.ds(pl.multiple_of(t * 8, 8), 8), :] = q
+                q = q + jnp.where(at[n], jnp.broadcast_to(cb[v // 2, x, f, w:w + 1, :], (8, 128)), 0.0)
             vals.append(q)
         res = list(acc)
         for v in range(8):
@@ -391,7 +411,7 @@
     ones8 = jnp.ones((8, 128), F32)
     ar[...] = lax.dot_general(ones8, gacc[...], (((1,), (1,)), ((), ())), precision=HI, preferred_element_type=F32)
 
-    def exchange(src, buf, me, first, dev):
+    def exchange(src, buf, me, first, dev, meanwhile):
         buf[me] = src[...]
         cps = []
         for d in range(1, 16):
@@ -399,6 +419,7 @@
             cp = rcopy(src, buf.at[me], as_s.at[first + d - 1], as_r.at[first + d - 1], b_, x_)
             cp.start()
             cps.append(cp)
+        meanwhile()
         for cp in cps:
             cp.wait_recv()
         drain.extend(cps)
@@ -407,8 +428,28 @@
             tot = [a + b_ for a, b_ in zip(tot[::2], tot[1::2])]
         return tot[0]
 
-    ar2[...] = exchange(ar, arx, z * NC + c, 0, zc)
-    ar3 = exchange(ar2, ary, (rho // NC) * NX + x, 15, yx)
+    def copies2(act):
+        n = 0
+        for src in range(NX):
+            for to in range(src + 1, NX):
+                act(n, src, to, lambda: rcopy(cb.at[src], cb2.at[src], cs2_s.at[n], cs2_r.at[n], blk, jnp.int32(to)))
+                n += 1
+
+    def start2(n, src, to, cp):
+        @pl.when(x == src)
+        def _():
+            cp().start()
+
+    def rest():
+        copies2(start2)
+
+        @pl.when(x == LATE[0][0])
+        def _():
+            move(0).wait_recv()
+        moves(LATE)
+
+    ar2[...] = exchange(ar, arx, z * NC + c, 0, zc, rest)
+    ar3 = exchange(ar2, ary, (rho // NC) * NX + x, 15, yx, lambda: None)
 
     r48 = lax.broadcasted_iota(jnp.int32, (48, 128), 0)
     l48 = lax.broadcasted_iota(jnp.int32, (48, 128), 1)
@@ -447,36 +488,70 @@
             upper = jnp.where(jnp.logical_and(iota8 == j, lane8 == i), jnp.broadcast_to(low[i, j], (8, 128)), upper)
     fac[...] = upper[:, 0:8]
 
-    def combine(i, _):
-        f, t = i // 8, lax.rem(i, 8)
-        rr = pl.ds(pl.multiple_of(t * 8, 8), 8)
-        vals = [gath[v, f, rr, :] for v in range(8)]
-        for v in range(8):
-            a = mix[pair(v, 0)] * vals[0]
-            for w in range(1, v + 1):
-                a = a + mix[pair(v, w)] * vals[w]
-            bas[v, f, rr, :] = a
-        return 0
-
-    lax.fori_loop(0, 40, combine, 0)
-    kq = lax.rem(x, 2)
-    homes = []
-    for v in range(2):
-        for d in (2, 1, 3):
-            cp = rcopy(bas.at[2 * xdev(d) + v], out.at[v, bq, :, kq], os.at[v, d - 1], orr.at[v, d - 1], blk, xdev(d))
-            cp.start()
-            homes.append(cp)
-    keep = []
-    for v in range(2):
-        cp = pltpu.make_async_copy(bas.at[2 * x + v], out.at[v, bq, :, kq], loc_sem.at[3 + v])
-        cp.start()
-        keep.append(cp)
-    for cp in keep:
-        cp.wait()
+    def combine_at(g):
+        for n in range(len(MOVES)):
+            if MOVES[n][3] == g and (g, MOVES[n]) != (3, MOVES[0]):
+                move(n).wait_recv()
+
+        def wait2(n, src, to, cp):
+            if to == g:
+                cp().wait_recv()
+
+        copies2(wait2)
+        odd_row = (iota8 & 1) == 1
+        for q in range(4):
+            def combine(f, _, q=q):
+                b, k = q // 2, q % 2
+                last = rows[b] - 1
+                fixes = []
+                for v in range(2):
+                    tot = zero8
+                    for src in range(g + 1):
+                        lo = mix[pair(2 * g + v, 2 * src)]
+                        hi = mix[pair(2 * g + v, 2 * src + 1)] if 2 * src + 1 <= 2 * g + v else 0.0
+                        rowsum = cb2[src, q, f] if src < g else cb[g, q, f]
+                        tot = tot + jnp.where(odd_row, hi, lo) * rowsum
+                    tot = tot + pltpu.roll(tot, 7, 0)
+                    fixes.append([jnp.broadcast_to(tot[r:r + 1], (8, 128)) for r in (0, 2, 4, 6)])
+                for t in range(8):
+                    vals = [gath[w // 2, q, w % 2, f, 8 * t:8 * t + 8, :] for w in range(2 * g + 2)]
+                    row = iota8 + 8 * t
+                    for v in range(2):
+                        a = mix[pair(2 * g + v, 0)] * vals[0]
+                        for w in range(1, 2 * g + v + 1):
+                            a = a + mix[pair(2 * g + v, w)] * vals[w]
+                        if t == 0:
+                            a = a + jnp.where(row == 0, fixes[v][0], 0.0) + jnp.where(row == 1, fixes[v][2], 0.0)
+                        if t >= 3:
+                            a = a + jnp.where(row == last, fixes[v][1], 0.0) + jnp.where(row == last - 1, fixes[v][3], 0.0)
+                        bas[v, b, f, k, 8 * t:8 * t + 8, :] = a
+                return 0
+
+            lax.fori_loop(0, NF, combine, 0)
+            for v in range(2):
+                pltpu.make_async_copy(bas.at[v, q // 2, :, q % 2], out.at[v, q // 2, :, q % 2], out_sem.at[v, q]).start()
+
+    for g in range(NX):
+        @pl.when(x == g)
+        def _():
+            combine_at(g)
+
     for cp in drain:
         cp.wait_send()
-    for cp in homes:
-        cp.wait()
+    for n in range(len(MOVES)):
+        @pl.when(x == MOVES[n][0])
+        def _():
+            move(n).wait_send()
+
+    def drain2(n, src, to, cp):
+        @pl.when(x == src)
+        def _():
+            cp().wait_send()
+
+    copies2(drain2)
+    for v in range(2):
+        for q in range(4):
+            pltpu.make_async_copy(bas.at[v, q // 2, :, q % 2], out.at[v, q // 2, :, q % 2], out_sem.at[v, q]).wait()
 
 
 def per_device(vectors, metric, jacobians, block_rows, neighbours, flipped):
@@ -497,9 +572,8 @@
             pltpu.SMEM((2, 2), jnp.int32),
             pltpu.VMEM((2, 2, NF, 2, 80, 128), F32),
             pltpu.VMEM((2, 2, NF, 2, 80, 128), F32),
-            pltpu.VMEM((4, 2, NF, 64, 128), F32),
-            pltpu.VMEM((8, NF, 64, 128), F32),
-            pltpu.VMEM((8, NF, 64, 128), F32),
+            pltpu.VMEM((4, 4, 2, NF, 64, 128), F32),
+            pltpu.VMEM(vectors.shape, F32),
             pltpu.VMEM((2, 4, 24, 128), F32),
             pltpu.VMEM((NZ, NC, 4, 24, 128), F32),
             pltpu.VMEM((NR, 8, 128), jnp.int32),
@@ -508,8 +582,8 @@
             pltpu.VMEM((NR, 4, 24, 128), F32),
             pltpu.VMEM((12, 16, 128), F32),
             pltpu.VMEM((12, 16, 128), F32),
-            pltpu.VMEM((4, NF, 8, 128), F32),
-            pltpu.VMEM((4, NF, 8, 128), F32),
+            pltpu.VMEM((4, 4, NF, 8, 128), F32),
+            pltpu.VMEM((4, 4, NF, 8, 128), F32),
             pltpu.VMEM((128, 128), F32),
             pltpu.VMEM((8, 128), F32),
             pltpu.VMEM((8, 128), F32),
@@ -517,14 +591,16 @@
             pltpu.VMEM((16, 8, 128), F32),
             pltpu.VMEM((48, 128), F32),
             pltpu.VMEM((36, 8, 128), F32),
-            dma((5,)), dma((5,)), dma((4,)),
+            dma((2,)), dma((5,)), dma((4,)),
             dma((2, 3)), dma((2, 3)),
             dma((17,)), dma((17,)),
             dma((7,)), dma((7,)),
             dma((7,)), dma((7,)),
             dma((3,)), dma((3,)),
             dma((30,)), dma((30,)),
-            dma((2, 3)), dma((2, 3)),
+            dma((len(MOVES),)), dma((len(MOVES),)),
+            dma((6,)), dma((6,)),
+            dma((2, 4)),
         ],
         compiler_params=pltpu.CompilerParams(collective_id=0, has_side_effects=True, vmem_limit_bytes=62 * 1024 * 1024),
         cost_estimate=pl.CostEstimate(flops=60_000_000, bytes_accessed=4_000_000, transcendentals=0),

time: 72 us -> 81.4 us (1.13)
  the two profiles are of different devices: /device:TPU:1 before, /device:TPU:4 now
where the time goes in v3:
time: 81.4 us; the launch traced here: 79.9 us
  Pallas kernels  76.2 us (94%)
  local copies, waits for them, and re-layouts  3.12 us (4%)
    pallas_call x1, Pallas kernels, per_device(): pl.pallas_call(kernel, out_shape=(jax.ShapeDtypeStruct(vectors.shape, F32...  76.2 us
    unnamed x4, local copies, waits for them, and re-layouts  3.12 us

profile of v3, /device:TPU:4, one launch (start us, length us, event | category | flops | bytes accessed | tf_op | source)
XLA Modules:
  0.0 79.9 jit_solution(11751029195833872516)
XLA Ops:
  0.6 76.2 %shard_map.77 = (f32[2,2,5,2,64,128]{5,4,3,2,1,0:T(8,128)}, f32[8,8]{1,0:T(8,128)}) custom-call(f32[2,2,5,2,64,128]{5,4,3,2,1,0:T(8,128)} %vec_h.1, f32[2,2,64,128]{3,2,1,0:T(8,128)} %met_h.1, f32[5,3,5]{2,1,0:T(4,128)} %bitcast.1, s32[2]{0:T(128)} %rows_h.1, s32[2,2]{1,0:T(2,128)} %nbr_h.1, s32[2,2]{1,0:T(2,128)} %flip_h.1), custom_call_target="tpu_custom_call" | custom-call | flops 60000000 | bytes 4000000 | tf_op jit(solution)/shard_map/pallas_call | solution.py:561
  76.8 0.0 copy-start
  76.8 2.5 %copy.10 = f32[2,2,5,2,64,128]{5,4,3,2,1,0:T(8,128)} copy(f32[2,2,5,2,64,128]{5,4,3,2,1,0:T(8,128)} %get-tuple-element.4) | data formatting | bytes 2621440
  79.4 0.0 copy-done
  79.4 0.6 copy.11
Async XLA Ops:
  76.8 2.5 %copy-start = (f32[8,8]{1,0:T(8,128)S(1)}, f32[8,8]{1,0:T(8,128)}, u32[]{:S(2)}) copy-start(f32[8,8]{1,0:T(8,128)} %get-tuple-element.5) | copy-start | bytes 772

commit v4 on v2

--- a/solution.py
+++ b/solution.py
@@ -16,13 +16,18 @@
 SCALE = 1024.0
 
 
+EARLY = [(1, 0, 2), (0, 3, 1), (0, 1, 3), (2, 1, 3)]
+LATE = [(0, 0, 2), (1, 1, 3)]
+MOVES = EARLY + LATE
+
+
 def pair(v, w):
     return v * (v + 1) // 2 + w
 
 
 def kernel(vec_h, met_h, jac_h, rows_h, nbr_h, flip_h, out, fac,
-           vec, met, jac, rows, nbr, flip, st, fi, se, gath, bas, pay, zb, rq, rqs, o2, rb, own, gst, cs, cb, gacc, ar, ar2, arx, ary, spl, mix,
-           loc_sem, in_sem, vec_sem, xs, xr, zs, zr, qs, qr, ys, yr, cs_s, cs_r, as_s, as_r, os, orr):
+           vec, met, jac, rows, nbr, flip, st, fi, gath, bas, res, pay, zb, rq, rqs, o2, rb, own, gst, cb, gacc, ar, ar2, arx, ary, spl, mix,
+           loc_sem, in_sem, vec_sem, xs, xr, zs, zr, qs, qr, ys, yr, cs_s, cs_r, as_s, as_r, ws, wr, cs2_s, cs2_r, os, orr, out_sem):
     blk = lax.axis_index("blk")
     x = lax.axis_index("vec")
     z = blk // NR
@@ -55,8 +60,8 @@
     def yc(d):
         return z * NR + lax.rem(rho + d, NR), x
 
-    partners = [zc(d) for d in range(1, 16)] + [yx(d) for d in range(1, 16)]
-    partners += [(z * NR + lax.rem(rho - c + NC * d, NR) + 1 - c, x) for d in range(1, NR // NC)]
+    partners = [(zdev(dz, core), x) for dz in (1, -1) for core in range(2)] + [yc(d) for d in range(1, NR)]
+    partners += [(blk, xdev(d)) for d in range(1, NX)]
     for b_, x_ in partners:
         pl.semaphore_signal(bar, inc=1, device_id={"blk": b_, "vec": x_}, device_id_type=MESH)
     n_part = len(partners)
@@ -196,7 +201,7 @@
             b, t = i // 8, lax.rem(i, 8)
 
             def store(f, k, val):
-                se[b * 2 + k, v, f, pl.ds(pl.multiple_of(t * 8, 8), 8), :] = val
+                gath[x, b * 2 + k, v, f, pl.ds(pl.multiple_of(t * 8, 8), 8), :] = val
 
             advance_tile(fi, v, b, t, SCALE, store)
             return 0
@@ -207,9 +212,27 @@
 
     def send_second(v):
         for d in (2, 1, 3):
-            cp = rcopy(se.at[xdev(d), v], gath.at[2 * x + v], xs.at[v, d - 1], xr.at[v, d - 1], blk, xdev(d))
+            here = gath.at[x, xdev(d), v]
+            cp = rcopy(here, here, xs.at[v, d - 1], xr.at[v, d - 1], blk, xdev(d))
             cp.start()
             sends.append(cp)
+
+    def move(n):
+        src, q, to = MOVES[n]
+        part = gath.at[src, q]
+        return rcopy(part, part, ws.at[n], wr.at[n], blk, jnp.int32(to))
+
+    def fix_move(n):
+        src, q, to = MOVES[n]
+        part = cb.at[src, q]
+        return rcopy(part, part, cs2_s.at[n], cs2_r.at[n], blk, jnp.int32(to))
+
+    def moves(make, which):
+        for n in range(len(MOVES)):
+            if MOVES[n] in which:
+                @pl.when(x == MOVES[n][0])
+                def _():
+                    make(n).start()
 
     second_pass(0)
     send_second(0)
@@ -237,9 +260,8 @@
     ring1 = ring_step(1, z_copies)
     second_pass(1)
     send_second(1)
+    moves(move, EARLY)
     ring2 = ring_step(2, ring1)
-    mygath = pltpu.make_async_copy(se.at[x], gath.at[pl.ds(2 * x, 2)], loc_sem.at[2])
-    mygath.start()
     for cp in q_copies:
         cp.wait_recv()
     tosmem = pltpu.make_async_copy(rq, rqs, loc_sem.at[1])
@@ -341,23 +363,26 @@
             near = VISC * c1[f] - sig * m1 * jmul(1, c1, f)
             face = face * SCALE
             near = near * SCALE
-            cs[b * 2, f, 0:4, :] = face[0:4]
-            cs[b * 2, f, 4:8, :] = near[0:4]
-            cs[b * 2 + 1, f, 0:4, :] = face[4:8]
-            cs[b * 2 + 1, f, 4:8, :] = near[4:8]
+            cb[x, b * 2, f, 0:4, :] = face[0:4]
+            cb[x, b * 2, f, 4:8, :] = near[0:4]
+            cb[x, b * 2 + 1, f, 0:4, :] = face[4:8]
+            cb[x, b * 2 + 1, f, 4:8, :] = near[4:8]
         s0, s1 = sums
         return s0 + jnp.where(odd == 0, total, 0.0), s1 + jnp.where(odd == 1, total, 0.0)
 
     ssq = lax.fori_loop(0, 2, fix, ssq)
     c_copies = []
     for d in (2, 1, 3):
-        cp = rcopy(cs.at[xdev(d)], cb.at[x], cs_s.at[d - 1], cs_r.at[d - 1], blk, xdev(d))
+        here = cb.at[x, xdev(d)]
+        cp = rcopy(here, here, cs_s.at[d - 1], cs_r.at[d - 1], blk, xdev(d))
         cp.start()
         c_copies.append(cp)
-    cb[x] = cs[x]
-
-    mygath.wait()
-    for cp in sends + c_copies:
+    moves(fix_move, MOVES)
+    moves(move, LATE)
+    for cp in sends:
+        cp.wait_recv()
+
+    for cp in c_copies:
         cp.wait_recv()
     drain += sends + c_copies
 
@@ -370,11 +395,10 @@
         at = [row == 0, row == my_last, row == 1, row == my_last - 1]
         vals = []
         for v in range(8):
-            q = gath[v, f, pl.ds(pl.multiple_of(t * 8, 8), 8), :]
+            q = gath[v // 2, x, v % 2, f, pl.ds(pl.multiple_of(t * 8, 8), 8), :]
             for n, (typ, side) in enumerate(((0, 0), (0, 1), (1, 0), (1, 1))):
                 w = typ * 4 + side * 2 + v % 2
-                q = q + jnp.where(at[n], jnp.broadcast_to(cb[v // 2, f, w:w + 1, :], (8, 128)), 0.0)
-            gath[v, f, pl.ds(pl.multiple_of(t * 8, 8), 8), :] = q
+                q = q + jnp.where(at[n], jnp.broadcast_to(cb[v // 2, x, f, w:w + 1, :], (8, 128)), 0.0)
             vals.append(q)
         res = list(acc)
         for v in range(8):
@@ -447,36 +471,89 @@
             upper = jnp.where(jnp.logical_and(iota8 == j, lane8 == i), jnp.broadcast_to(low[i, j], (8, 128)), upper)
     fac[...] = upper[:, 0:8]
 
-    def combine(i, _):
-        f, t = i // 8, lax.rem(i, 8)
-        rr = pl.ds(pl.multiple_of(t * 8, 8), 8)
-        vals = [gath[v, f, rr, :] for v in range(8)]
-        for v in range(8):
-            a = mix[pair(v, 0)] * vals[0]
-            for w in range(1, v + 1):
-                a = a + mix[pair(v, w)] * vals[w]
-            bas[v, f, rr, :] = a
-        return 0
-
-    lax.fori_loop(0, 40, combine, 0)
-    kq = lax.rem(x, 2)
-    homes = []
-    for v in range(2):
-        for d in (2, 1, 3):
-            cp = rcopy(bas.at[2 * xdev(d) + v], out.at[v, bq, :, kq], os.at[v, d - 1], orr.at[v, d - 1], blk, xdev(d))
-            cp.start()
-            homes.append(cp)
-    keep = []
-    for v in range(2):
-        cp = pltpu.make_async_copy(bas.at[2 * x + v], out.at[v, bq, :, kq], loc_sem.at[3 + v])
-        cp.start()
-        keep.append(cp)
-    for cp in keep:
-        cp.wait()
+    odd_row = (iota8 & 1) == 1
+
+    def combine(q, outs, put):
+        top = max(outs) // 2 + 1
+
+        def body(f, _):
+            last = rows[q // 2] - 1
+            fixes = []
+            for o in outs:
+                tot = zero8
+                for src in range(o // 2 + 1):
+                    lo = mix[pair(o, 2 * src)]
+                    hi = mix[pair(o, 2 * src + 1)] if 2 * src + 1 <= o else 0.0
+                    tot = tot + jnp.where(odd_row, hi, lo) * cb[src, q, f]
+                tot = tot + pltpu.roll(tot, 7, 0)
+                fixes.append([jnp.broadcast_to(tot[r:r + 1], (8, 128)) for r in (0, 2, 4, 6)])
+            for t in range(8):
+                vals = [gath[w // 2, q, w % 2, f, 8 * t:8 * t + 8, :] for w in range(2 * top)]
+                row = iota8 + 8 * t
+                for n, o in enumerate(outs):
+                    a = mix[pair(o, 0)] * vals[0]
+                    for w in range(1, o + 1):
+                        a = a + mix[pair(o, w)] * vals[w]
+                    if t == 0:
+                        a = a + jnp.where(row == 0, fixes[n][0], 0.0) + jnp.where(row == 1, fixes[n][2], 0.0)
+                    if t >= 3:
+                        a = a + jnp.where(row == last, fixes[n][1], 0.0) + jnp.where(row == last - 1, fixes[n][3], 0.0)
+                    put(n, f, t, a)
+            return 0
+
+        lax.fori_loop(0, NF, body, 0)
+
+    def home(i, v, q, to):
+        return rcopy(res.at[i, v], out.at[v, q // 2, :, q % 2], os.at[i, v], orr.at[i, v], blk, jnp.int32(to))
+
+    def own_copy(v, q):
+        there = out.at[v, q // 2, :, q % 2]
+        return pltpu.make_async_copy(bas.at[v, q // 2, :, q % 2], there, out_sem.at[v, q])
+
+    def finish(g):
+        beside = [(i, (g + d) % NX) for i, d in ((0, 1), (1, -1)) if (g + d) % NX > 0]
+        for i, to in beside:
+            def put(n, f, t, a, i=i):
+                res[i, n, f, 8 * t:8 * t + 8, :] = a
+
+            combine(g, [2 * to, 2 * to + 1], put)
+            for v in range(2):
+                home(i, v, g, to).start()
+        mine_q = [g, (g + 2) % NX] if g > 0 else [0, 1, 2, 3]
+        for q in mine_q:
+            if q != g:
+                for n in range(len(MOVES)):
+                    if MOVES[n][1:] == (q, g):
+                        move(n).wait_recv()
+                        fix_move(n).wait_recv()
+
+            def put_own(n, f, t, a, q=q):
+                bas[n, q // 2, f, q % 2, 8 * t:8 * t + 8, :] = a
+
+            combine(q, [2 * g, 2 * g + 1], put_own)
+            for v in range(2):
+                own_copy(v, q).start()
+        for n in range(len(MOVES)):
+            if MOVES[n][0] == g:
+                move(n).wait_send()
+                fix_move(n).wait_send()
+        for q in mine_q:
+            for v in range(2):
+                own_copy(v, q).wait()
+        for i, to in beside:
+            for v in range(2):
+                home(i, v, g, to).wait_send()
+        if g > 0:
+            for i, frm in ((0, (g - 1) % NX), (1, (g + 1) % NX)):
+                for v in range(2):
+                    home(i, v, frm, g).wait_recv()
+
     for cp in drain:
         cp.wait_send()
-    for cp in homes:
-        cp.wait()
+    for g in range(NX):
+        @pl.when(x == g)
+        def _():
+            finish(g)
 
 
 def per_device(vectors, metric, jacobians, block_rows, neighbours, flipped):
@@ -497,9 +574,9 @@
             pltpu.SMEM((2, 2), jnp.int32),
             pltpu.VMEM((2, 2, NF, 2, 80, 128), F32),
             pltpu.VMEM((2, 2, NF, 2, 80, 128), F32),
-            pltpu.VMEM((4, 2, NF, 64, 128), F32),
-            pltpu.VMEM((8, NF, 64, 128), F32),
-            pltpu.VMEM((8, NF, 64, 128), F32),
+            pltpu.VMEM((4, 4, 2, NF, 64, 128), F32),
+            pltpu.VMEM(vectors.shape, F32),
+            pltpu.VMEM((2, 2, NF, 64, 128), F32),
             pltpu.VMEM((2, 4, 24, 128), F32),
             pltpu.VMEM((NZ, NC, 4, 24, 128), F32),
             pltpu.VMEM((NR, 8, 128), jnp.int32),
@@ -508,8 +585,7 @@
             pltpu.VMEM((NR, 4, 24, 128), F32),
             pltpu.VMEM((12, 16, 128), F32),
             pltpu.VMEM((12, 16, 128), F32),
-            pltpu.VMEM((4, NF, 8, 128), F32),
-            pltpu.VMEM((4, NF, 8, 128), F32),
+            pltpu.VMEM((4, 4, NF, 8, 128), F32),
             pltpu.VMEM((128, 128), F32),
             pltpu.VMEM((8, 128), F32),
             pltpu.VMEM((8, 128), F32),
@@ -517,14 +593,17 @@
             pltpu.VMEM((16, 8, 128), F32),
             pltpu.VMEM((48, 128), F32),
             pltpu.VMEM((36, 8, 128), F32),
-            dma((5,)), dma((5,)), dma((4,)),
+            dma((2,)), dma((5,)), dma((4,)),
             dma((2, 3)), dma((2, 3)),
             dma((17,)), dma((17,)),
             dma((7,)), dma((7,)),
             dma((7,)), dma((7,)),
             dma((3,)), dma((3,)),
             dma((30,)), dma((30,)),
-            dma((2, 3)), dma((2, 3)),
+            dma((len(MOVES),)), dma((len(MOVES),)),
+            dma((6,)), dma((6,)),
+            dma((2, 2)), dma((2, 2)),
+            dma((2, 4)),
         ],
         compiler_params=pltpu.CompilerParams(collective_id=0, has_side_effects=True, vmem_limit_bytes=62 * 1024 * 1024),
         cost_estimate=pl.CostEstimate(flops=60_000_000, bytes_accessed=4_000_000, transcendentals=0),

time: 72 us -> 71.7 us (level)
  the two profiles are of different devices: /device:TPU:1 before, /device:TPU:4 now
where the time goes in v4:
time: 71.7 us; the launch traced here: 70.9 us
  Pallas kernels  67.1 us (94%)
  local copies, waits for them, and re-layouts  3.12 us (4%)
    pallas_call x1, Pallas kernels, per_device(): pl.pallas_call(kernel, out_shape=(jax.ShapeDtypeStruct(vectors.shape, F32...  67.1 us
    unnamed x4, local copies, waits for them, and re-layouts  3.12 us

profile of v4, /device:TPU:4, one launch (start us, length us, event | category | flops | bytes accessed | tf_op | source)
XLA Modules:
  0.0 70.9 jit_solution(13300016676784582325)
XLA Ops:
  0.6 67.1 %shard_map.77 = (f32[2,2,5,2,64,128]{5,4,3,2,1,0:T(8,128)}, f32[8,8]{1,0:T(8,128)}) custom-call(f32[2,2,5,2,64,128]{5,4,3,2,1,0:T(8,128)} %vec_h.1, f32[2,2,64,128]{3,2,1,0:T(8,128)} %met_h.1, f32[5,3,5]{2,1,0:T(4,128)} %bitcast.1, s32[2]{0:T(128)} %rows_h.1, s32[2,2]{1,0:T(2,128)} %nbr_h.1, s32[2,2]{1,0:T(2,128)} %flip_h.1), custom_call_target="tpu_custom_call" | custom-call | flops 60000000 | bytes 4000000 | tf_op jit(solution)/shard_map/pallas_call | solution.py:563
  67.7 0.0 copy-start
  67.7 2.5 %copy.10 = f32[2,2,5,2,64,128]{5,4,3,2,1,0:T(8,128)} copy(f32[2,2,5,2,64,128]{5,4,3,2,1,0:T(8,128)} %get-tuple-element.4) | data formatting | bytes 2621440
  70.3 0.0 copy-done
  70.3 0.6 copy.11
Async XLA Ops:
  67.7 2.5 %copy-start = (f32[8,8]{1,0:T(8,128)S(1)}, f32[8,8]{1,0:T(8,128)}, u32[]{:S(2)}) copy-start(f32[8,8]{1,0:T(8,128)} %get-tuple-element.5) | copy-start | bytes 772

commit v5 on v4

--- a/solution.py
+++ b/solution.py
@@ -74,6 +74,92 @@
     iota8 = lax.broadcasted_iota(jnp.int32, (8, 128), 0)
     lane8 = lax.broadcasted_iota(jnp.int32, (8, 128), 1)
     zero8 = jnp.zeros((8, 128), F32)
+
+    for cp in small + big:
+        cp.wait()
+
+    sig = jnp.where((iota8 >> 1) & 1 == 0, -1.0, 1.0)
+    sk = jnp.where(iota8 < 4, 1.0, -1.0)
+    odd = iota8 & 1
+
+    def jmul(d, g_, f):
+        acc = jac[f, d, 0] * g_[0]
+        for g in range(1, NF):
+            acc = acc + jac[f, d, g] * g_[g]
+        return acc
+
+    def faces(i, _):
+        b, side, v = i // 4, lax.rem(i // 2, 2), lax.rem(i, 2)
+        last = jnp.maximum(rows[b] - 1, 1)
+        r = jnp.where(side == 0, 0, last)
+        adj = jnp.where(side == 0, 1, last - 1)
+        slot = b * 2 + side
+        lane_row = b * 8 + side * 2 + v
+        for f in range(NF):
+            for k in range(2):
+                a = vec[v, b, f, k, pl.ds(r, 1), :]
+                pay[v, slot, f * 2 + k:f * 2 + k + 1, :] = a
+                own[f, pl.ds(lane_row + 4 * k, 1), :] = a
+                gst[f, pl.ds(lane_row + 4 * k, 1), :] = vec[v, b, f, k, pl.ds(adj, 1), :]
+        for k in range(2):
+            m = met[b, k, pl.ds(r, 1), :]
+            pay[v, slot, 20 + k:21 + k, :] = m
+            pay[v, slot, 22 + k:23 + k, :] = m
+            own[10, pl.ds(lane_row + 4 * k, 1), :] = m
+            own[11, pl.ds(lane_row + 4 * k, 1), :] = met[b, k, pl.ds(adj, 1), :]
+        return 0
+
+    lax.fori_loop(0, 8, faces, 0)
+
+    def face_step(b, _):
+        base = pl.ds(pl.multiple_of(b * 8, 8), 8)
+        q = [own[f, base, :] for f in range(NF)]
+        near = [gst[f, base, :] for f in range(NF)]
+        m0 = own[10, base, :]
+        e = [pltpu.roll(a, 127, 1) for a in q]
+        w = [pltpu.roll(a, 1, 1) for a in q]
+        ok = [pltpu.roll(a, 4, 0) for a in q]
+        ew = [a - b_ for a, b_ in zip(e, w)]
+        for f in range(NF):
+            flux = jmul(0, ew, f) + sk * jmul(2, ok, f) - sig * jmul(1, near, f)
+            own[NF + f, base, :] = (1.0 - 6.0 * VISC) * q[f] + VISC * (e[f] + w[f] + ok[f] + near[f]) - m0 * flux
+        return 0
+
+    lax.fori_loop(0, 2, face_step, 0)
+
+    def pack(i, _):
+        b, side, v = i // 4, lax.rem(i // 2, 2), lax.rem(i, 2)
+        lane_row = b * 8 + side * 2 + v
+        for f in range(NF):
+            for k in range(2):
+                pay[v, b * 2 + side, 10 + f * 2 + k:11 + f * 2 + k, :] = own[NF + f, pl.ds(lane_row + 4 * k, 1), :]
+        return 0
+
+    lax.fori_loop(0, 8, pack, 0)
+    req = jnp.where(lane8 == 0, nbr[0, 0], jnp.where(lane8 == 1, nbr[0, 1], jnp.where(lane8 == 2, nbr[1, 0], nbr[1, 1])))
+    rq[rho] = req
+
+    pl.semaphore_wait(bar, n_part)
+
+    mine = pltpu.make_async_copy(pay.at[c], zb.at[z, c], loc_sem.at[0])
+    mine.start()
+    z_copies = []
+    for j in range(2):
+        core = lax.rem(c + j, NC)
+        for h in range(2):
+            for side, dz in ((0, 1), (1, -1)):
+                n = j * 4 + h * 2 + side
+                half = pl.ds(2 * h, 2)
+                cp = rcopy(pay.at[core, half], zb.at[z, c, half], zs.at[n], zr.at[n], zdev(dz, core), x)
+                cp.start()
+                z_copies.append(cp)
+    other = rcopy(pay.at[1 - c], zb.at[z, c], zs.at[8], zr.at[8], zdev(0, 1 - c), x)
+    other.start()
+    q_copies = []
+    for d in range(1, NR):
+        cp = rcopy(rq.at[rho], rq.at[rho], qs.at[d - 1], qr.at[d - 1], z * NR + lax.rem(rho + d, NR), x)
+        cp.start()
+        q_copies.append(cp)
 
     def fill(i, _):
         vb = i // 10
@@ -88,12 +174,7 @@
         fi[v, b, f, k, 72:80, :] = zero8
         return 0
 
-    small[0].wait()
-    for n in range(4):
-        big[n].wait()
-        lax.fori_loop(10 * n, 10 * n + 10, fill, 0)
-    for cp in small[1:]:
-        cp.wait()
+    lax.fori_loop(0, 40, fill, 0)
 
     def advance_tile(src, v, b, t, scale, store):
         r0 = pl.multiple_of(t * 8, 8)
@@ -149,53 +230,6 @@
 
     ssq = lax.fori_loop(0, 32, first_pass, (zero8, zero8))
 
-    def faces(i, _):
-        b, side, v = i // 4, lax.rem(i // 2, 2), lax.rem(i, 2)
-        last = jnp.maximum(rows[b] - 1, 1)
-        r = jnp.where(side == 0, 0, last)
-        adj = jnp.where(side == 0, 1, last - 1)
-        slot = b * 2 + side
-        lane_row = b * 8 + side * 2 + v
-        for f in range(NF):
-            for k in range(2):
-                a = st[v, b, f, k, pl.ds(r + 8, 1), :]
-                p = fi[v, b, f, k, pl.ds(r + 8, 1), :]
-                pay[v, slot, f * 2 + k:f * 2 + k + 1, :] = a
-                pay[v, slot, 10 + f * 2 + k:11 + f * 2 + k, :] = p
-                own[f, pl.ds(lane_row + 4 * k, 1), :] = a
-                own[NF + f, pl.ds(lane_row + 4 * k, 1), :] = p
-        for k in range(2):
-            m = met[b, k, pl.ds(r, 1), :]
-            pay[v, slot, 20 + k:21 + k, :] = m
-            pay[v, slot, 22 + k:23 + k, :] = m
-            own[10, pl.ds(lane_row + 4 * k, 1), :] = m
-            own[11, pl.ds(lane_row + 4 * k, 1), :] = met[b, k, pl.ds(adj, 1), :]
-        return 0
-
-    lax.fori_loop(0, 8, faces, 0)
-    req = jnp.where(lane8 == 0, nbr[0, 0], jnp.where(lane8 == 1, nbr[0, 1], jnp.where(lane8 == 2, nbr[1, 0], nbr[1, 1])))
-    rq[rho] = req
-
-    pl.semaphore_wait(bar, n_part)
-
-    mine = pltpu.make_async_copy(pay.at[c], zb.at[z, c], loc_sem.at[0])
-    mine.start()
-    z_copies = []
-    for j in range(2):
-        core = lax.rem(c + j, NC)
-        for side, dz in ((0, 1), (1, -1)):
-            n = j * 2 + side
-            cp = rcopy(pay.at[core], zb.at[z, c], zs.at[n], zr.at[n], zdev(dz, core), x)
-            cp.start()
-            z_copies.append(cp)
-    other = rcopy(pay.at[1 - c], zb.at[z, c], zs.at[4], zr.at[4], zdev(0, 1 - c), x)
-    other.start()
-    q_copies = []
-    for d in range(1, NR):
-        cp = rcopy(rq.at[rho], rq.at[rho], qs.at[d - 1], qr.at[d - 1], z * NR + lax.rem(rho + d, NR), x)
-        cp.start()
-        q_copies.append(cp)
-
     def second_pass(v):
         def body(i, _):
             b, t = i // 8, lax.rem(i, 8)
@@ -234,33 +268,32 @@
                 def _():
                     make(n).start()
 
-    second_pass(0)
-    send_second(0)
-
     drain = z_copies + [other]
 
     def ring_step(s, before):
         cps = []
         for j in range(2):
             core = lax.rem(c + j, NC)
-            for side, dz in ((0, 1), (1, -1)):
-                if s == 3 and side != j:
-                    before[j * 2 + side].wait_recv()
-                    continue
-                n = 5 + (s - 1) * 4 + j * 2 + side
-                slot = lax.rem(z - dz * s + NZ, NZ)
-                part = zb.at[slot, core]
-                before[j * 2 + side].wait_recv()
-                cp = rcopy(part, part, zs.at[n], zr.at[n], zdev(dz, c), x)
-                cp.start()
-                cps.append(cp)
+            for h in range(2):
+                for side, dz in ((0, 1), (1, -1)):
+                    m = j * 4 + h * 2 + side
+                    before[m].wait_recv()
+                    if s == 3 and side != j:
+                        continue
+                    n = 9 + (s - 1) * 8 + m
+                    part = zb.at[lax.rem(z - dz * s + NZ, NZ), core, pl.ds(2 * h, 2)]
+                    cp = rcopy(part, part, zs.at[n], zr.at[n], zdev(dz, c), x)
+                    cp.start()
+                    cps.append(cp)
         drain.extend(cps)
         return cps
 
     ring1 = ring_step(1, z_copies)
+    second_pass(0)
+    send_second(0)
+
     second_pass(1)
     send_second(1)
-    moves(move, EARLY)
     ring2 = ring_step(2, ring1)
     for cp in q_copies:
         cp.wait_recv()
@@ -320,16 +353,6 @@
         return 0
 
     lax.fori_loop(0, 8, unpack, 0)
-
-    sig = jnp.where((iota8 >> 1) & 1 == 0, -1.0, 1.0)
-    sk = jnp.where(iota8 < 4, 1.0, -1.0)
-    odd = iota8 & 1
-
-    def jmul(d, g_, f):
-        acc = jac[f, d, 0] * g_[0]
-        for g in range(1, NF):
-            acc = acc + jac[f, d, g] * g_[g]
-        return acc
 
     def fix(b, sums):
         base = pl.ds(pl.multiple_of(b * 8, 8), 8)
@@ -378,7 +401,7 @@
         cp.start()
         c_copies.append(cp)
     moves(fix_move, MOVES)
-    moves(move, LATE)
+    moves(move, EARLY)
     for cp in sends:
         cp.wait_recv()
 
@@ -415,7 +438,7 @@
     ones8 = jnp.ones((8, 128), F32)
     ar[...] = lax.dot_general(ones8, gacc[...], (((1,), (1,)), ((), ())), precision=HI, preferred_element_type=F32)
 
-    def exchange(src, buf, me, first, dev):
+    def exchange(src, buf, me, first, dev, then):
         buf[me] = src[...]
         cps = []
         for d in range(1, 16):
@@ -423,6 +446,7 @@
             cp = rcopy(src, buf.at[me], as_s.at[first + d - 1], as_r.at[first + d - 1], b_, x_)
             cp.start()
             cps.append(cp)
+        then()
         for cp in cps:
             cp.wait_recv()
         drain.extend(cps)
@@ -431,8 +455,8 @@
             tot = [a + b_ for a, b_ in zip(tot[::2], tot[1::2])]
         return tot[0]
 
-    ar2[...] = exchange(ar, arx, z * NC + c, 0, zc)
-    ar3 = exchange(ar2, ary, (rho // NC) * NX + x, 15, yx)
+    ar2[...] = exchange(ar, arx, z * NC + c, 0, zc, lambda: None)
+    ar3 = exchange(ar2, ary, (rho // NC) * NX + x, 15, yx, lambda: moves(move, LATE))
 
     r48 = lax.broadcasted_iota(jnp.int32, (48, 128), 0)
     l48 = lax.broadcasted_iota(jnp.int32, (48, 128), 1)
@@ -562,7 +586,7 @@
     dma = pltpu.SemaphoreType.DMA
     return pl.pallas_call(
         kernel,
-        out_shape=(jax.ShapeDtypeStruct(vectors.shape, F32), jax.ShapeDtypeStruct((8, 8), F32)),
+        out_shape=(pltpu.VMEM(vectors.shape, F32), jax.ShapeDtypeStruct((8, 8), F32)),
         in_specs=[hbm] * 6,
         out_specs=(pl.BlockSpec(memory_space=pl.ANY), vm),
         scratch_shapes=[
@@ -595,7 +619,7 @@
             pltpu.VMEM((36, 8, 128), F32),
             dma((2,)), dma((5,)), dma((4,)),
             dma((2, 3)), dma((2, 3)),
-            dma((17,)), dma((17,)),
+            dma((33,)), dma((33,)),
             dma((7,)), dma((7,)),
             dma((7,)), dma((7,)),
             dma((3,)), dma((3,)),
@@ -605,7 +629,7 @@
             dma((2, 2)), dma((2, 2)),
             dma((2, 4)),
         ],
-        compiler_params=pltpu.CompilerParams(collective_id=0, has_side_effects=True, vmem_limit_bytes=62 * 1024 * 1024),
+        compiler_params=pltpu.CompilerParams(collective_id=0, has_side_effects=True, vmem_limit_bytes=60 * 1024 * 1024),
         cost_estimate=pl.CostEstimate(flops=60_000_000, bytes_accessed=4_000_000, transcendentals=0),
     )(vectors, metric, jnp.transpose(jacobians, (1, 0, 2)), block_rows, neighbours, flipped)
 

time: 71.7 us -> 63.1 us (0.88)
  Pallas kernels: 67.1 us -> 60.4 us
  local copies, waits for them, and re-layouts: 3.12 us -> 1.66 us
    pallas_call x1, Pallas kernels: 67.1 us -> 60.4 us  [per_device(): pl.pallas_call(kernel, out_shape=(pltpu.VMEM(vectors.shape, F32), jax.Sha...]
    unnamed x4, local copies, waits for them, and re-layouts: 3.12 us -> 1.66 us
where the time goes in v5:
time: 63.1 us; the launch traced here: 62.7 us
  Pallas kernels  60.4 us (96%)
  local copies, waits for them, and re-layouts  1.66 us (3%)
  between operations  0.65 us (1%)
    pallas_call x1, Pallas kernels, per_device(): pl.pallas_call(kernel, out_shape=(pltpu.VMEM(vectors.shape, F32), jax.Sha...  60.4 us
    unnamed x4, local copies, waits for them, and re-layouts  1.66 us

profile of v5, /device:TPU:4, one launch (start us, length us, event | category | flops | bytes accessed | tf_op | source)
XLA Modules:
  0.0 62.7 jit_solution(5633021128491918647)
XLA Ops:
  0.6 60.4 %shard_map.77 = (f32[2,2,5,2,64,128]{5,4,3,2,1,0:T(8,128)S(1)}, f32[8,8]{1,0:T(8,128)}) custom-call(f32[2,2,5,2,64,128]{5,4,3,2,1,0:T(8,128)} %vec_h.1, f32[2,2,64,128]{3,2,1,0:T(8,128)} %met_h.1, f32[5,3,5]{2,1,0:T(4,128)} %bitcast.1, s32[2]{0:T(128)} %rows_h.1, s32[2,2]{1,0:T(2,128)} %nbr_h.1, s32[2,2]{1,0:T(2,128)} %flip_h.1), custom_call_target="tpu_custom_call" | custom-call | flops 60000000 | bytes 4000000 | tf_op jit(solution)/shard_map/pallas_call | solution.py:587
  61.1 0.0 copy-start
  61.1 1.1 %copy.10 = f32[2,2,5,2,64,128]{5,4,3,2,1,0:T(8,128)} copy(f32[2,2,5,2,64,128]{5,4,3,2,1,0:T(8,128)S(1)} %get-tuple-element.2) | data formatting | bytes 2621440
  62.2 0.0 copy-done
  62.2 0.6 copy.11
Async XLA Ops:
  61.1 1.1 %copy-start = (f32[8,8]{1,0:T(8,128)S(1)}, f32[8,8]{1,0:T(8,128)}, u32[]{:S(2)}) copy-start(f32[8,8]{1,0:T(8,128)} %get-tuple-element.7) | copy-start | bytes 772

commit v6 on v5

--- a/solution.py
+++ b/solution.py
@@ -17,8 +17,8 @@
 
 
 EARLY = [(1, 0, 2), (0, 3, 1), (0, 1, 3), (2, 1, 3)]
-LATE = [(0, 0, 2), (1, 1, 3)]
-MOVES = EARLY + LATE
+FAR = [(0, 0, 2), (1, 1, 3)]
+MOVES = EARLY + FAR
 
 
 def pair(v, w):
@@ -26,7 +26,7 @@
 
 
 def kernel(vec_h, met_h, jac_h, rows_h, nbr_h, flip_h, out, fac,
-           vec, met, jac, rows, nbr, flip, st, fi, gath, bas, res, pay, zb, rq, rqs, o2, rb, own, gst, cb, gacc, ar, ar2, arx, ary, spl, mix,
+           vec, met, jac, rows, nbr, flip, st, fi, gath, bas, res, pay, zb, rq, rqs, o2, rb, own, gst, cb, edge, near, gacc, ar, ar2, arx, ary, spl, mix,
            loc_sem, in_sem, vec_sem, xs, xr, zs, zr, qs, qr, ys, yr, cs_s, cs_r, as_s, as_r, ws, wr, cs2_s, cs2_r, os, orr, out_sem):
     blk = lax.axis_index("blk")
     x = lax.axis_index("vec")
@@ -114,15 +114,15 @@
     def face_step(b, _):
         base = pl.ds(pl.multiple_of(b * 8, 8), 8)
         q = [own[f, base, :] for f in range(NF)]
-        near = [gst[f, base, :] for f in range(NF)]
+        inside = [gst[f, base, :] for f in range(NF)]
         m0 = own[10, base, :]
         e = [pltpu.roll(a, 127, 1) for a in q]
         w = [pltpu.roll(a, 1, 1) for a in q]
         ok = [pltpu.roll(a, 4, 0) for a in q]
         ew = [a - b_ for a, b_ in zip(e, w)]
         for f in range(NF):
-            flux = jmul(0, ew, f) + sk * jmul(2, ok, f) - sig * jmul(1, near, f)
-            own[NF + f, base, :] = (1.0 - 6.0 * VISC) * q[f] + VISC * (e[f] + w[f] + ok[f] + near[f]) - m0 * flux
+            flux = jmul(0, ew, f) + sk * jmul(2, ok, f) - sig * jmul(1, inside, f)
+            own[NF + f, base, :] = (1.0 - 6.0 * VISC) * q[f] + VISC * (e[f] + w[f] + ok[f] + inside[f]) - m0 * flux
         return 0
 
     lax.fori_loop(0, 2, face_step, 0)
@@ -174,7 +174,7 @@
         fi[v, b, f, k, 72:80, :] = zero8
         return 0
 
-    lax.fori_loop(0, 40, fill, 0)
+    lax.fori_loop(0, 20, fill, 0)
 
     def advance_tile(src, v, b, t, scale, store):
         r0 = pl.multiple_of(t * 8, 8)
@@ -228,7 +228,7 @@
         s0, s1 = sums
         return s0 + jnp.where(v == 0, sq, 0.0), s1 + jnp.where(v == 1, sq, 0.0)
 
-    ssq = lax.fori_loop(0, 32, first_pass, (zero8, zero8))
+    ssq = lax.fori_loop(0, 16, first_pass, (zero8, zero8))
 
     def second_pass(v):
         def body(i, _):
@@ -251,22 +251,29 @@
             cp.start()
             sends.append(cp)
 
-    def move(n):
+    def move(n, v):
         src, q, to = MOVES[n]
-        part = gath.at[src, q]
-        return rcopy(part, part, ws.at[n], wr.at[n], blk, jnp.int32(to))
+        part = gath.at[src, q, v]
+        return rcopy(part, part, ws.at[n, v], wr.at[n, v], blk, jnp.int32(to))
 
     def fix_move(n):
         src, q, to = MOVES[n]
         part = cb.at[src, q]
         return rcopy(part, part, cs2_s.at[n], cs2_r.at[n], blk, jnp.int32(to))
 
-    def moves(make, which):
+    def moves(which, vs):
         for n in range(len(MOVES)):
             if MOVES[n] in which:
                 @pl.when(x == MOVES[n][0])
                 def _():
-                    make(n).start()
+                    for v in vs:
+                        move(n, v).start()
+
+    def fix_moves():
+        for n in range(len(MOVES)):
+            @pl.when(x == MOVES[n][0])
+            def _():
+                fix_move(n).start()
 
     drain = z_copies + [other]
 
@@ -288,12 +295,15 @@
         drain.extend(cps)
         return cps
 
-    ring1 = ring_step(1, z_copies)
     second_pass(0)
     send_second(0)
+    ring1 = ring_step(1, z_copies)
+    lax.fori_loop(20, 40, fill, 0)
+    ssq = lax.fori_loop(16, 32, first_pass, ssq)
 
     second_pass(1)
     send_second(1)
+    moves(FAR, (0,))
     ring2 = ring_step(2, ring1)
     for cp in q_copies:
         cp.wait_recv()
@@ -400,43 +410,61 @@
         cp = rcopy(here, here, cs_s.at[d - 1], cs_r.at[d - 1], blk, xdev(d))
         cp.start()
         c_copies.append(cp)
-    moves(fix_move, MOVES)
-    moves(move, EARLY)
+    fix_moves()
+    moves(EARLY, (0, 1))
     for cp in sends:
         cp.wait_recv()
 
+    bq = x // 2
+    my_last = jnp.where(bq == 0, rows[0], rows[1]) - 1
+    safe_last = jnp.maximum(my_last, 1)
+
+    def products(acc, left, right):
+        res = list(acc)
+        for v in range(8):
+            for w in range(v + 1):
+                res[pair(v, w)] = res[pair(v, w)] + left[v] * right[w]
+        return tuple(res)
+
+    def gram_tile(i, acc):
+        f, t = i // 8, lax.rem(i, 8)
+        row = iota8 + t * 8
+        inner = jnp.logical_and(row > 1, jnp.logical_or(row < my_last - 1, row > my_last))
+        vals = [gath[v // 2, x, v % 2, f, pl.ds(pl.multiple_of(t * 8, 8), 8), :] for v in range(8)]
+        for v in range(8):
+            near[v, f, pl.ds(pl.multiple_of(t * 8, 8), 8), :] = vals[v]
+        return products(acc, [jnp.where(inner, q, 0.0) for q in vals], vals)
+
+    grams = lax.fori_loop(0, 40, gram_tile, tuple(zero8 for _ in range(36)))
+
+    def edges(i, _):
+        f, v = i // 8, lax.rem(i, 8)
+        for j, r in enumerate((0, safe_last, 1, safe_last - 1)):
+            edge[v // 2, f, pl.ds(2 * j + lax.rem(v, 2), 1), :] = near[v, f, pl.ds(r, 1), :]
+        return 0
+
+    lax.fori_loop(0, 40, edges, 0)
     for cp in c_copies:
         cp.wait_recv()
     drain += sends + c_copies
-
-    bq = x // 2
-    my_last = jnp.where(bq == 0, rows[0], rows[1]) - 1
-
-    def gram_tile(i, acc):
-        f, t = i // 8, lax.rem(i, 8)
-        row = iota8 + t * 8
-        at = [row == 0, row == my_last, row == 1, row == my_last - 1]
+    odd_row = (iota8 & 1) == 1
+
+    def gram_edge(f, acc):
         vals = []
-        for v in range(8):
-            q = gath[v // 2, x, v % 2, f, pl.ds(pl.multiple_of(t * 8, 8), 8), :]
-            for n, (typ, side) in enumerate(((0, 0), (0, 1), (1, 0), (1, 1))):
-                w = typ * 4 + side * 2 + v % 2
-                q = q + jnp.where(at[n], jnp.broadcast_to(cb[v // 2, x, f, w:w + 1, :], (8, 128)), 0.0)
-            vals.append(q)
-        res = list(acc)
-        for v in range(8):
-            for w in range(v + 1):
-                res[pair(v, w)] = res[pair(v, w)] + vals[v] * vals[w]
-        return tuple(res)
-
-    grams = lax.fori_loop(0, 40, gram_tile, tuple(zero8 for _ in range(36)))
+        for src in range(NX):
+            both = edge[src, f] + cb[src, x, f]
+            vals.append(jnp.where(odd_row, 0.0, both))
+            vals.append(jnp.where(odd_row, 0.0, pltpu.roll(both, 7, 0)))
+        return products(acc, vals, vals)
+
+    grams = lax.fori_loop(0, NF, gram_edge, grams)
     gacc[...] = jnp.zeros((128, 128), F32)
     for n in range(36):
         gacc[n:n + 1, :] = jnp.sum(grams[n], axis=0, keepdims=True)
     for v in range(2):
         gacc[pl.ds(36 + 2 * x + v, 1), :] = jnp.sum(ssq[v], axis=0, keepdims=True)
     ones8 = jnp.ones((8, 128), F32)
-    ar[...] = lax.dot_general(ones8, gacc[...], (((1,), (1,)), ((), ())), precision=HI, preferred_element_type=F32)
+    ar[...] = lax.dot_general(ones8, gacc[...], (((1,), (1,)), ((), ())), precision=HI, preferred_element_type=F32)[0:1, :]
 
     def exchange(src, buf, me, first, dev, then):
         buf[me] = src[...]
@@ -456,7 +484,7 @@
         return tot[0]
 
     ar2[...] = exchange(ar, arx, z * NC + c, 0, zc, lambda: None)
-    ar3 = exchange(ar2, ary, (rho // NC) * NX + x, 15, yx, lambda: moves(move, LATE))
+    ar3 = exchange(ar2, ary, (rho // NC) * NX + x, 15, yx, lambda: moves(FAR, (1,)))
 
     r48 = lax.broadcasted_iota(jnp.int32, (48, 128), 0)
     l48 = lax.broadcasted_iota(jnp.int32, (48, 128), 1)
@@ -495,8 +523,6 @@
             upper = jnp.where(jnp.logical_and(iota8 == j, lane8 == i), jnp.broadcast_to(low[i, j], (8, 128)), upper)
     fac[...] = upper[:, 0:8]
 
-    odd_row = (iota8 & 1) == 1
-
     def combine(q, outs, put):
         top = max(outs) // 2 + 1
 
@@ -548,7 +574,8 @@
             if q != g:
                 for n in range(len(MOVES)):
                     if MOVES[n][1:] == (q, g):
-                        move(n).wait_recv()
+                        move(n, 0).wait_recv()
+                        move(n, 1).wait_recv()
                         fix_move(n).wait_recv()
 
             def put_own(n, f, t, a, q=q):
@@ -559,7 +586,8 @@
                 own_copy(v, q).start()
         for n in range(len(MOVES)):
             if MOVES[n][0] == g:
-                move(n).wait_send()
+                move(n, 0).wait_send()
+                move(n, 1).wait_send()
                 fix_move(n).wait_send()
         for q in mine_q:
             for v in range(2):
@@ -610,11 +638,13 @@
             pltpu.VMEM((12, 16, 128), F32),
             pltpu.VMEM((12, 16, 128), F32),
             pltpu.VMEM((4, 4, NF, 8, 128), F32),
+            pltpu.VMEM((4, NF, 8, 128), F32),
+            pltpu.VMEM((8, NF, 64, 128), F32),
             pltpu.VMEM((128, 128), F32),
-            pltpu.VMEM((8, 128), F32),
-            pltpu.VMEM((8, 128), F32),
-            pltpu.VMEM((16, 8, 128), F32),
-            pltpu.VMEM((16, 8, 128), F32),
+            pltpu.VMEM((1, 128), F32),
+            pltpu.VMEM((1, 128), F32),
+            pltpu.VMEM((16, 1, 128), F32),
+            pltpu.VMEM((16, 1, 128), F32),
             pltpu.VMEM((48, 128), F32),
             pltpu.VMEM((36, 8, 128), F32),
             dma((2,)), dma((5,)), dma((4,)),
@@ -624,7 +654,7 @@
             dma((7,)), dma((7,)),
             dma((3,)), dma((3,)),
             dma((30,)), dma((30,)),
-            dma((len(MOVES),)), dma((len(MOVES),)),
+            dma((len(MOVES), 2)), dma((len(MOVES), 2)),
             dma((6,)), dma((6,)),
             dma((2, 2)), dma((2, 2)),
             dma((2, 4)),

time: 63.1 us -> 59.3 us (0.940)
  Pallas kernels: 60.4 us -> 56.9 us
    pallas_call x1, Pallas kernels: 60.4 us -> 56.9 us  [per_device(): pl.pallas_call(kernel, out_shape=(pltpu.VMEM(vectors.shape, F32), jax.Sha...]
where the time goes in v6:
time: 59.3 us; the launch traced here: 59.2 us
  Pallas kernels  56.9 us (96%)
  local copies, waits for them, and re-layouts  1.66 us (3%)
  between operations  0.65 us (1%)
    pallas_call x1, Pallas kernels, per_device(): pl.pallas_call(kernel, out_shape=(pltpu.VMEM(vectors.shape, F32), jax.Sha...  56.9 us
    unnamed x4, local copies, waits for them, and re-layouts  1.66 us

profile of v6, /device:TPU:4, one launch (start us, length us, event | category | flops | bytes accessed | tf_op | source)
XLA Modules:
  0.0 59.2 jit_solution(17301535867447370282)
XLA Ops:
  0.6 56.9 %shard_map.77 = (f32[2,2,5,2,64,128]{5,4,3,2,1,0:T(8,128)S(1)}, f32[8,8]{1,0:T(8,128)}) custom-call(f32[2,2,5,2,64,128]{5,4,3,2,1,0:T(8,128)} %vec_h.1, f32[2,2,64,128]{3,2,1,0:T(8,128)} %met_h.1, f32[5,3,5]{2,1,0:T(4,128)} %bitcast.1, s32[2]{0:T(128)} %rows_h.1, s32[2,2]{1,0:T(2,128)} %nbr_h.1, s32[2,2]{1,0:T(2,128)} %flip_h.1), custom_call_target="tpu_custom_call" | custom-call | flops 60000000 | bytes 4000000 | tf_op jit(solution)/shard_map/pallas_call | solution.py:615
  57.5 0.0 copy-start
  57.5 1.1 %copy.10 = f32[2,2,5,2,64,128]{5,4,3,2,1,0:T(8,128)} copy(f32[2,2,5,2,64,128]{5,4,3,2,1,0:T(8,128)S(1)} %get-tuple-element.2) | data formatting | bytes 2621440
  58.6 0.0 copy-done
  58.6 0.6 %copy.11 = f32[8,8]{1,0:T(8,128)} copy(f32[8,8]{1,0:T(8,128)S(1)} %copy-done) | data formatting | bytes 512
Async XLA Ops:
  57.5 1.1 %copy-start = (f32[8,8]{1,0:T(8,128)S(1)}, f32[8,8]{1,0:T(8,128)}, u32[]{:S(2)}) copy-start(f32[8,8]{1,0:T(8,128)} %get-tuple-element.7) | copy-start | bytes 772

commit v7 on v6

--- a/solution.py
+++ b/solution.py
@@ -323,13 +323,14 @@
         o2[to, r] = zb[bid >> 4, (bid >> 1) & 1, (bid & 1) * 2 + (1 - side)]
         return 0
 
-    lax.fori_loop(0, 4 * NR, pick, 0)
     y_copies = []
-    for d in range(1, NR):
+    for d in (4, 5, 3, 2, 6, 1, 7):
         to = lax.rem(rho + d, NR)
+        lax.fori_loop(4 * to, 4 * to + 4, pick, 0)
         cp = rcopy(o2.at[to], rb.at[rho], ys.at[d - 1], yr.at[d - 1], z * NR + to, x)
         cp.start()
         y_copies.append(cp)
+    lax.fori_loop(4 * rho, 4 * rho + 4, pick, 0)
     rb[rho] = o2[rho]
     for cp in y_copies:
         cp.wait_recv()

time: 59.3 us -> 57.3 us (0.966)
  Pallas kernels: 56.9 us -> 54.6 us
    pallas_call x1, Pallas kernels: 56.9 us -> 54.6 us  [per_device(): pl.pallas_call(kernel, out_shape=(pltpu.VMEM(vectors.shape, F32), jax.Sha...]
where the time goes in v7:
time: 57.3 us; the launch traced here: 56.9 us
  Pallas kernels  54.6 us (95%)
  local copies, waits for them, and re-layouts  1.66 us (3%)
  between operations  0.65 us (1%)
    pallas_call x1, Pallas kernels, per_device(): pl.pallas_call(kernel, out_shape=(pltpu.VMEM(vectors.shape, F32), jax.Sha...  54.6 us
    unnamed x4, local copies, waits for them, and re-layouts  1.66 us

profile of v7, /device:TPU:4, one launch (start us, length us, event | category | flops | bytes accessed | tf_op | source)
XLA Modules:
  0.0 56.9 jit_solution(5146103866584330703)
XLA Ops:
  0.6 54.6 %shard_map.77 = (f32[2,2,5,2,64,128]{5,4,3,2,1,0:T(8,128)S(1)}, f32[8,8]{1,0:T(8,128)}) custom-call(f32[2,2,5,2,64,128]{5,4,3,2,1,0:T(8,128)} %vec_h.1, f32[2,2,64,128]{3,2,1,0:T(8,128)} %met_h.1, f32[5,3,5]{2,1,0:T(4,128)} %bitcast.1, s32[2]{0:T(128)} %rows_h.1, s32[2,2]{1,0:T(2,128)} %nbr_h.1, s32[2,2]{1,0:T(2,128)} %flip_h.1), custom_call_target="tpu_custom_call" | custom-call | flops 60000000 | bytes 4000000 | tf_op jit(solution)/shard_map/pallas_call | solution.py:616
  55.3 0.0 copy-start
  55.3 1.1 %copy.10 = f32[2,2,5,2,64,128]{5,4,3,2,1,0:T(8,128)} copy(f32[2,2,5,2,64,128]{5,4,3,2,1,0:T(8,128)S(1)} %get-tuple-element.2) | data formatting | bytes 2621440
  56.3 0.0 copy-done
  56.3 0.6 %copy.11 = f32[8,8]{1,0:T(8,128)} copy(f32[8,8]{1,0:T(8,128)S(1)} %copy-done) | data formatting | bytes 512
Async XLA Ops:
  55.3 1.1 %copy-start = (f32[8,8]{1,0:T(8,128)S(1)}, f32[8,8]{1,0:T(8,128)}, u32[]{:S(2)}) copy-start(f32[8,8]{1,0:T(8,128)} %get-tuple-element.7) | copy-start | bytes 772

commit v8 on v7

--- a/solution.py
+++ b/solution.py
@@ -561,8 +561,12 @@
         there = out.at[v, q // 2, :, q % 2]
         return pltpu.make_async_copy(bas.at[v, q // 2, :, q % 2], there, out_sem.at[v, q])
 
+    def targets(g):
+        beside = [(i, (g + d) % NX) for i, d in ((0, 1), (1, -1)) if (g + d) % NX > 0]
+        return beside, [g, (g + 2) % NX] if g > 0 else [0, 1, 2, 3]
+
     def finish(g):
-        beside = [(i, (g + d) % NX) for i, d in ((0, 1), (1, -1)) if (g + d) % NX > 0]
+        beside, mine_q = targets(g)
         for i, to in beside:
             def put(n, f, t, a, i=i):
                 res[i, n, f, 8 * t:8 * t + 8, :] = a
@@ -570,7 +574,6 @@
             combine(g, [2 * to, 2 * to + 1], put)
             for v in range(2):
                 home(i, v, g, to).start()
-        mine_q = [g, (g + 2) % NX] if g > 0 else [0, 1, 2, 3]
         for q in mine_q:
             if q != g:
                 for n in range(len(MOVES)):
@@ -585,6 +588,9 @@
             combine(q, [2 * g, 2 * g + 1], put_own)
             for v in range(2):
                 own_copy(v, q).start()
+
+    def settle(g):
+        beside, mine_q = targets(g)
         for n in range(len(MOVES)):
             if MOVES[n][0] == g:
                 move(n, 0).wait_send()
@@ -601,12 +607,17 @@
                 for v in range(2):
                     home(i, v, frm, g).wait_recv()
 
+    for g in range(NX):
+        @pl.when(x == g)
+        def _():
+            finish(g)
+
     for cp in drain:
         cp.wait_send()
     for g in range(NX):
         @pl.when(x == g)
         def _():
-            finish(g)
+            settle(g)
 
 
 def per_device(vectors, metric, jacobians, block_rows, neighbours, flipped):

time: 57.3 us -> 57.2 us (level)
  no operation moved by 1% of the time
where the time goes in v8:
time: 57.2 us; the launch traced here: 56.9 us
  Pallas kernels  54.6 us (95%)
  local copies, waits for them, and re-layouts  1.66 us (3%)
  between operations  0.65 us (1%)
    pallas_call x1, Pallas kernels, per_device(): pl.pallas_call(kernel, out_shape=(pltpu.VMEM(vectors.shape, F32), jax.Sha...  54.6 us
    unnamed x4, local copies, waits for them, and re-layouts  1.66 us

profile of v8, /device:TPU:4, one launch (start us, length us, event | category | flops | bytes accessed | tf_op | source)
XLA Modules:
  0.0 56.9 jit_solution(7100661502587906774)
XLA Ops:
  0.6 54.6 %shard_map.77 = (f32[2,2,5,2,64,128]{5,4,3,2,1,0:T(8,128)S(1)}, f32[8,8]{1,0:T(8,128)}) custom-call(f32[2,2,5,2,64,128]{5,4,3,2,1,0:T(8,128)} %vec_h.1, f32[2,2,64,128]{3,2,1,0:T(8,128)} %met_h.1, f32[5,3,5]{2,1,0:T(4,128)} %bitcast.1, s32[2]{0:T(128)} %rows_h.1, s32[2,2]{1,0:T(2,128)} %nbr_h.1, s32[2,2]{1,0:T(2,128)} %flip_h.1), custom_call_target="tpu_custom_call" | custom-call | flops 60000000 | bytes 4000000 | tf_op jit(solution)/shard_map/pallas_call | solution.py:627
  55.3 0.0 copy-start
  55.3 1.1 %copy.10 = f32[2,2,5,2,64,128]{5,4,3,2,1,0:T(8,128)} copy(f32[2,2,5,2,64,128]{5,4,3,2,1,0:T(8,128)S(1)} %get-tuple-element.2) | data formatting | bytes 2621440
  56.3 0.0 copy-done
  56.3 0.6 %copy.11 = f32[8,8]{1,0:T(8,128)} copy(f32[8,8]{1,0:T(8,128)S(1)} %copy-done) | data formatting | bytes 512
Async XLA Ops:
  55.3 1.1 %copy-start = (f32[8,8]{1,0:T(8,128)S(1)}, f32[8,8]{1,0:T(8,128)}, u32[]{:S(2)}) copy-start(f32[8,8]{1,0:T(8,128)} %get-tuple-element.7) | copy-start | bytes 772

commit v9 on v7

--- a/solution.py
+++ b/solution.py
@@ -470,7 +470,7 @@
     def exchange(src, buf, me, first, dev, then):
         buf[me] = src[...]
         cps = []
-        for d in range(1, 16):
+        for d in (8, 10, 9, 7, 6, 11, 5, 2, 14, 12, 4, 13, 3, 1, 15):
             b_, x_ = dev(d)
             cp = rcopy(src, buf.at[me], as_s.at[first + d - 1], as_r.at[first + d - 1], b_, x_)
             cp.start()

time: 57.3 us -> 57.3 us (level)
  no operation moved by 1% of the time
where the time goes in v9:
time: 57.3 us; the launch traced here: 56.9 us
  Pallas kernels  54.6 us (95%)
  local copies, waits for them, and re-layouts  1.66 us (3%)
  between operations  0.65 us (1%)
    pallas_call x1, Pallas kernels, per_device(): pl.pallas_call(kernel, out_shape=(pltpu.VMEM(vectors.shape, F32), jax.Sha...  54.6 us
    unnamed x4, local copies, waits for them, and re-layouts  1.66 us

profile of v9, /device:TPU:4, one launch (start us, length us, event | category | flops | bytes accessed | tf_op | source)
XLA Modules:
  0.0 56.9 jit_solution(5431083311675867197)
XLA Ops:
  0.6 54.6 %shard_map.77 = (f32[2,2,5,2,64,128]{5,4,3,2,1,0:T(8,128)S(1)}, f32[8,8]{1,0:T(8,128)}) custom-call(f32[2,2,5,2,64,128]{5,4,3,2,1,0:T(8,128)} %vec_h.1, f32[2,2,64,128]{3,2,1,0:T(8,128)} %met_h.1, f32[5,3,5]{2,1,0:T(4,128)} %bitcast.1, s32[2]{0:T(128)} %rows_h.1, s32[2,2]{1,0:T(2,128)} %nbr_h.1, s32[2,2]{1,0:T(2,128)} %flip_h.1), custom_call_target="tpu_custom_call" | custom-call | flops 60000000 | bytes 4000000 | tf_op jit(solution)/shard_map/pallas_call | solution.py:616
  55.3 0.0 copy-start
  55.3 1.1 %copy.10 = f32[2,2,5,2,64,128]{5,4,3,2,1,0:T(8,128)} copy(f32[2,2,5,2,64,128]{5,4,3,2,1,0:T(8,128)S(1)} %get-tuple-element.2) | data formatting | bytes 2621440
  56.3 0.0 copy-done
  56.3 0.6 %copy.11 = f32[8,8]{1,0:T(8,128)} copy(f32[8,8]{1,0:T(8,128)S(1)} %copy-done) | data formatting | bytes 512
Async XLA Ops:
  55.3 1.1 %copy-start = (f32[8,8]{1,0:T(8,128)S(1)}, f32[8,8]{1,0:T(8,128)}, u32[]{:S(2)}) copy-start(f32[8,8]{1,0:T(8,128)} %get-tuple-element.7) | copy-start | bytes 772
